TPU v7x, 128 devices: a whole 4x4x4 slice. The times are simulated.
128 devices in a mesh: row: 8 (over x, y_hi), col: 16 (over y_lo, z, core).
Axes of the slice: x: 4, y: 4 (y_hi: 2, y_lo: 2; y = y_hi * 2 + y_lo), z: 4, core: 2. Of those that a mesh axis runs over, the one named last changes fastest.
Arguments:
- tokens: bfloat16 [1024, 12288], P('col', 'row'), may hold values from -6 to 6
- w_in: bfloat16 [12288, 49152], P('row', 'col'), may hold values from -0.0546875 to 0.0546875
- b_in: bfloat16 [49152], P('col'), may hold values from -3 to 3
- w_out: bfloat16 [49152, 12288], P('col', 'row'), may hold values from -0.02734375 to 0.02734375
- b_out: bfloat16 [12288], P('row'), may hold values from -3 to 3
Outputs:
- output_rows: float32 [1024, 12288], P('col', 'row')
All inputs are finite; a program needn't handle non-finite values.
Results may differ from a plain program's by a relative error of at most 0.0024.
Values may be sent and summed in bfloat16 or wider, within the bound.
A program may use at most 128 MiB of HBM per device.

v0:
```python
import jax
import jax.numpy as jnp
from jax import lax
from jax.sharding import PartitionSpec as P


def per_device(tokens, w_in, b_in, w_out, b_out):
    partial_value = jnp.dot(
        lax.all_gather(tokens, "col", axis=0, tiled=True), w_in, preferred_element_type=jnp.float32
    )
    in_bias = b_in.astype(jnp.float32)
    own_rows = lax.psum_scatter(partial_value, "row", scatter_dimension=0, tiled=True)
    hidden = jax.nn.gelu(own_rows + in_bias, approximate=True).astype(jnp.bfloat16)
    out_partial = jnp.dot(
        lax.all_gather(hidden, "row", axis=0, tiled=True), w_out, preferred_element_type=jnp.float32
    )
    output_rows = lax.psum_scatter(out_partial, "col", scatter_dimension=0, tiled=True)
    return output_rows + b_out.astype(jnp.float32)


def solution(mesh):
    return jax.shard_map(
        per_device,
        mesh=mesh,
        in_specs=(P("col", "row"), P("row", "col"), P("col"), P("col", "row"), P("row")),
        out_specs=P("col", "row"),
        check_vma=False,
    )
```

profile of v0, /device:TPU:1, one launch (start us, length us, event | category | flops | bytes accessed | tf_op | source)
XLA Modules:
  0.0 395.4 jit_solution(7046318448082981294)
XLA Ops:
  6.5 0.0 all-gather.3.cloned.1.call-start
  6.5 0.7 all-gather.3.cloned.1.call-update
  7.3 0.0 reduce-scatter.3.cloned.1.call-start
  7.3 41.5 %all-gather.3.cloned.1.call-done = bf16[1024,1536]{1,0:T(8,128)(2,1)} async-done(((bf16[64,1536]{1,0:T(8,128)(2,1)}), bf16[1024,1536]{1,0:T(8,128)(2,1)}) %all-gather.3.cloned.1.call-update) | async-done | bytes 3145744 | tf_op jit(solution)/shard_map/all_gather | solution.py:9
  48.8 16.2 %fusion.8 = f32[1024,3072]{1,0:T(8,128)} fusion(bf16[1024,1536]{1,0:T(8,128)(2,1)} %all-gather.3.cloned.1.call-done, bf16[1536,3072]{1,0:T(8,128)(2,1)} %param.6), kind=kOutput, calls=%fused_computation.10 | convolution fusion | flops 9663676416 | bytes 25165824 | tf_op jit(solution)/shard_map/dot_general | solution.py:8
  64.9 0.0 copy-start
  64.9 0.0 reduce-scatter.3.cloned.1.call-update
  65.0 0.0 all-gather.5.cloned.1.call-start
  65.0 0.6 copy-done
  65.6 150.0 %reduce-scatter.3.cloned.1.call-done = f32[128,3072]{1,0:T(8,128)} async-done(((f32[1024,3072]{1,0:T(8,128)}), f32[128,3072]{1,0:T(8,128)}) %reduce-scatter.3.cloned.1.call-update) | async-done | bytes 1572880 | tf_op jit(solution)/shard_map/reduce_scatter | solution.py:12
  215.7 2.9 fusion.7
  218.5 0.0 all-gather.5.cloned.1.call-update
  218.6 0.0 reduce-scatter.5.cloned.1.call-start
  218.6 87.7 %all-gather.5.cloned.1.call-done = bf16[1024,3072]{1,0:T(8,128)(2,1)} async-done(((bf16[128,3072]{1,0:T(8,128)(2,1)}), bf16[1024,3072]{1,0:T(8,128)(2,1)}) %all-gather.5.cloned.1.call-update) | async-done | bytes 6291472 | tf_op jit(solution)/shard_map/all_gather | solution.py:15
  306.3 15.4 %fusion.9 = f32[1024,1536]{1,0:T(8,128)} fusion(bf16[1024,3072]{1,0:T(8,128)(2,1)} %all-gather.5.cloned.1.call-done, bf16[3072,1536]{1,0:T(8,128)(2,1)} %param.8), kind=kOutput, calls=%fused_computation.11 | convolution fusion | flops 9663676416 | bytes 22020096 | tf_op jit(solution)/shard_map/dot_general | solution.py:14
  321.7 0.0 copy-start.1
  321.7 0.0 reduce-scatter.5.cloned.1.call-update
  321.7 0.7 copy-done.1
  322.4 64.7 %reduce-scatter.5.cloned.1.call-done = f32[64,1536]{1,0:T(8,128)} async-done(((f32[1024,1536]{1,0:T(8,128)}), f32[64,1536]{1,0:T(8,128)}) %reduce-scatter.5.cloned.1.call-update) | async-done | bytes 393232 | tf_op jit(solution)/shard_map/reduce_scatter | solution.py:17
  387.1 1.8 broadcast_add_fusion
  (2 shorter events, 0.0 us)
Async XLA Ops:
  6.5 42.2 %all-gather.3.cloned.1.call-start = ((), (), s32[]{:S(2)}) async-start(), calls=%async_computation.2 | async-start | bytes 3342336 | tf_op jit(solution)/shard_map/all_gather | solution.py:9
  7.3 208.4 %reduce-scatter.3.cloned.1.call-start = ((), (), s32[]{:S(2)}) async-start(), calls=%async_computation.3 | async-start | bytes 14155776 | tf_op jit(solution)/shard_map/reduce_scatter | solution.py:12
  64.9 0.7 copy-start
  65.0 241.3 %all-gather.5.cloned.1.call-start = ((), (), s32[]{:S(2)}) async-start(), calls=%async_computation.4 | async-start | bytes 7077888 | tf_op jit(solution)/shard_map/all_gather | solution.py:15
  218.6 168.5 %reduce-scatter.5.cloned.1.call-start = ((), (), s32[]{:S(2)}) async-start(), calls=%async_computation.5 | async-start | bytes 6684672 | tf_op jit(solution)/shard_map/reduce_scatter | solution.py:17
  321.7 0.7 copy-start.1
Sparse Core Ops, SparseCore 0:
  9.1 39.6 all-gather.2
  65.1 150.5 reduce-scatter.2
  218.7 87.5 all-gather.4
  321.9 65.1 reduce-scatter.4
where the time goes:
time: 399 us; the launch traced here: 395 us
  waiting for transfers between devices  345 us (86%)
  matrix products  31.5 us (8%)
  between operations  13.1 us (3%)
  other arithmetic  4.63 us (1%)
    reduce_scatter x1, waiting for transfers between devices, per_device(): lax.psum_scatter(partial_value, 'row', scatter_dimension=0, tiled=True)  150 us
    all_gather x1, waiting for transfers between devices, per_device(): lax.all_gather(hidden, 'row', axis=0, tiled=True)  87.7 us
    reduce_scatter x1, waiting for transfers between devices, per_device(): lax.psum_scatter(out_partial, 'col', scatter_dimension=0, tiled=True)  64.7 us
    all_gather x1, waiting for transfers between devices, per_device(): lax.all_gather(tokens, 'col', axis=0, tiled=True)  41.5 us
    dot_general x1, matrix products, per_device(): jnp.dot(lax.all_gather(tokens, 'col', axis=0, tiled=True), w_in, preferre...  16.2 us
    dot_general x1, matrix products, per_device(): jnp.dot(lax.all_gather(hidden, 'row', axis=0, tiled=True), w_out, preferr...  15.4 us
  transfers between devices with their start and end apart: 4, of which 4 were waited for; matrix products, arithmetic and copies ran while one was open for 0% of the time, Pallas kernels for 0%

commit v1 on v0

v1 whole, which is shorter than its diff:
```python
import jax
import jax.numpy as jnp
from jax import lax
from jax.experimental import pallas as pl
from jax.experimental.pallas import tpu as pltpu
from jax.sharding import PartitionSpec as P

MESH = pl.DeviceIdType.MESH
F32, BF16 = jnp.float32, jnp.bfloat16
CHUNKS = 8
ROWS, HALF = 128, 64
D, FF = 1536, 3072
PAIR, QUARTER = 768, 384

ORDER = (
    ("first", 0), ("pass_on", -1), ("sum_y", 1), ("gather_x", 2), ("second", 3), ("sum_x", 0),
    ("activate", 1), ("gather_xx", 2), ("send_out", 3), ("cross", 4),
)
STEPS = CHUNKS + 3


def kernel(tok_hbm, w1_hbm, bin_ref, w2_hbm, bout_ref, out_ref,
           w1, w2, tok, x1s, x1r, keep1, x2s, x2r, keep2, ys, yr, keep3, hid, po, cr, osend, orecv, y2s, y2r,
           w1_sem, w2_sem, own_sem, tok_ss, tok_rs, fwd_ss, fwd_rs, first_ss, relay_ss,
           x1_ss, x1_rs, x2_ss, x2_rs, y_ss, y_rs, gy_ss, gy_rs, gx_ss, gx_rs, gxx_ss, gxx_rs,
           c_ss, c_rs, o_ss, o_rs, y2_ss, y2_rs):
    row, col = lax.axis_index("row"), lax.axis_index("col")
    x, yh = row // 2, row % 2
    yl, z, core = col // 8, (col // 2) % 4, col % 2
    x_one = x + 1 - 2 * (x % 2)
    x_three = 3 - x
    one = (x_one * 2 + yh, col)
    three = (x_three * 2 + yh, col)
    across = (x * 2 + 1 - yh, col)
    sibling = (row, col + 1 - 2 * core)
    low = (row, (1 - yl) * 8 + z * 2 + core)

    def along_z(d):
        return (row, yl * 8 + ((z + d) % 4) * 2 + core)

    mine = (((x + 1) // 2) % 2, x // 2)
    q = (x // 2, x % 2)
    pair_of = tuple(h * 2 * PAIR + mine[h] * PAIR for h in (0, 1))
    other_pair = tuple(h * 2 * PAIR + (1 - mine[h]) * PAIR for h in (0, 1))
    quarter_of = tuple(pair_of[h] + q[h] * QUARTER for h in (0, 1))
    my_block = quarter_of[0] * (1 - yh) + quarter_of[1] * yh
    dest1, dest2 = (one, three), (three, one)

    def cols(start, size):
        return pl.ds(pl.multiple_of(start, 128), size)

    def remote(src, dst, ss, rs, dev):
        return pltpu.make_async_remote_copy(src_ref=src, dst_ref=dst, send_sem=ss, recv_sem=rs, device_id=dev, device_id_type=MESH)

    w1_order = (other_pair[0], other_pair[1], pair_of[0], pair_of[1])

    def load_w1(i):
        c = cols(w1_order[i], PAIR)
        return pltpu.make_async_copy(w1_hbm.at[:, c], w1.at[:, c], w1_sem.at[i])

    own_rows = pl.ds(pl.multiple_of(core * HALF, HALF), HALF)
    other_rows = pl.ds(pl.multiple_of((1 - core) * HALF, HALF), HALF)
    own = pltpu.make_async_copy(tok_hbm, tok.at[0, own_rows], own_sem)
    own.start()
    for i in range(4):
        load_w1(i).start()
    load_w2 = pltpu.make_async_copy(w2_hbm, w2, w2_sem)
    load_w2.start()

    barrier = pltpu.get_barrier_semaphore()
    partners = [one, three, across, sibling, low] + [along_z(d) for d in (1, 2, 3)]
    for dev in partners:
        pl.semaphore_signal(barrier, inc=1, device_id=dev, device_id_type=MESH)
    pl.semaphore_wait(barrier, len(partners))

    def token_slot(t):
        return tok.at[t, own_rows]

    def to_sibling(t):
        return remote(token_slot(t), token_slot(t), fwd_ss.at[t], fwd_rs.at[t], sibling)

    def from_sibling(t):
        return remote(tok.at[t, other_rows], tok.at[t, other_rows], fwd_ss.at[t], fwd_rs.at[t], sibling)

    own.wait()
    to_sibling(0).start()
    to_low = remote(token_slot(0), token_slot(1), first_ss.at[0], tok_rs.at[1], low)
    to_low.start()
    to_z = []
    for d in (1, 3, 2):
        copy = remote(token_slot(0), token_slot(4 + d), first_ss.at[d], tok_rs.at[4 + d], along_z(4 - d))
        copy.start()
        to_z.append(copy)

    def relay(d):
        return remote(token_slot(1), token_slot(1 + d), relay_ss.at[d - 1], tok_rs.at[1 + d], along_z(4 - d))

    def pass_on(t):
        remote(token_slot(t), token_slot(t), tok_ss.at[0], tok_rs.at[t], low).wait_recv()
        to_sibling(t).start()

        @pl.when(t == 1)
        def _():
            for d in (1, 3, 2):
                relay(d).start()

    def x1_copy(t, h):
        return remote(x1s.at[t % 2, h], x1r.at[t, h], x1_ss.at[t % 2, h], x1_rs.at[t, h], dest1[h])

    def first(t):
        from_sibling(t).wait_recv()
        for i in range(4):
            h = i % 2

            @pl.when(t == 0)
            def _():
                load_w1(i).wait()

            if i < 2:
                @pl.when(t >= 2)
                def _():
                    x1_copy(t, h).wait_send()

            part = jnp.dot(tok[t], w1[:, cols(w1_order[i], PAIR)], preferred_element_type=F32)
            if i < 2:
                x1s[t % 2, h] = part.astype(BF16)
                x1_copy(t, h).start()
            else:
                keep1[h] = part

    def x2_copy(t, h):
        return remote(x2s.at[t % 2, h], x2r.at[t, h], x2_ss.at[t % 2, h], x2_rs.at[t, h], dest2[h])

    def sum_x(t):
        for h in (0, 1):
            x1_copy(t, h).wait_recv()

            @pl.when(t >= 2)
            def _():
                x2_copy(t, h).wait_send()

            gone = cols((1 - q[h]) * QUARTER, QUARTER)
            x2s[t % 2, h] = (keep1[h, :, gone] + x1r[t, h, :, gone].astype(F32)).astype(BF16)
            x2_copy(t, h).start()
        for h in (0, 1):
            kept = cols(q[h] * QUARTER, QUARTER)
            keep2[h] = keep1[h, :, kept] + x1r[t, h, :, kept].astype(F32)

    def y_copy(t):
        return remote(ys.at[t % 2], yr.at[t], y_ss.at[t % 2], y_rs.at[t], across)

    def sum_y(t):
        for h in (0, 1):
            x2_copy(t, h).wait_recv()

        @pl.when(t >= 2)
        def _():
            y_copy(t).wait_send()

        ys[t % 2] = keep2[1 - yh] + x2r[t, 1 - yh].astype(F32)
        y_copy(t).start()
        keep3[...] = keep2[yh] + x2r[t, yh].astype(F32)

    def hid_copy(t, start, size, ss, rs, dev):
        c = cols(start, size)
        return remote(hid.at[t, :, c], hid.at[t, :, c], ss, rs, dev)

    def gy_copy(t):
        return hid_copy(t, my_block, QUARTER, gy_ss.at[t], gy_rs.at[t], across)

    def gx_copy(t, h):
        return hid_copy(t, quarter_of[h], QUARTER, gx_ss.at[t, h], gx_rs.at[t, h], dest2[h])

    def gxx_copy(t, h):
        return hid_copy(t, pair_of[h], PAIR, gxx_ss.at[t, h], gxx_rs.at[t, h], dest1[h])

    def activate(t):
        y_copy(t).wait_recv()
        c = cols(my_block, QUARTER)
        hid[t, :, c] = jax.nn.gelu(keep3[...] + yr[t] + bin_ref[:, c], approximate=True).astype(BF16)
        gy_copy(t).start()

    def gather_x(t):
        gy_copy(t).wait_recv()
        for h in (0, 1):
            gx_copy(t, h).start()

    def gather_xx(t):
        for h in (0, 1):
            gx_copy(t, h).wait_recv()
            gxx_copy(t, h).start()

    def c_copy(t):
        return remote(po.at[t % 2, other_rows], cr.at[t], c_ss.at[t % 2], c_rs.at[t], sibling)

    def second(t):
        @pl.when(t == 0)
        def _():
            load_w2.wait()

        @pl.when(t >= 2)
        def _():
            c_copy(t).wait_send()

        for h in (0, 1):
            gxx_copy(t, h).wait_recv()
        for i in range(2):
            c = pl.ds(i * PAIR, PAIR)
            po[t % 2, :, c] = jnp.dot(hid[t], w2[:, c], preferred_element_type=F32)
        c_copy(t).start()

    def o_copy(t):
        far = (t + 3) // 4 % 2
        return remote(osend.at[t % 2], orecv.at[t], o_ss.at[t % 2], o_rs.at[t], along_z((t + 3 * far) % 4))

    def send_out(t):
        c_copy(t).wait_recv()

        @pl.when(t < 2)
        def _():
            orecv[t] = po[t % 2, own_rows] + cr[t]

        @pl.when(t >= 2)
        def _():
            @pl.when(t >= 4)
            def _():
                o_copy(t).wait_send()

            osend[t % 2] = po[t % 2, own_rows] + cr[t]
            o_copy(t).start()

    y2_copy = remote(y2s, y2r, y2_ss, y2_rs, low)

    def cross(t):
        @pl.when(t == 4)
        def _():
            for i in (2, 3, 4):
                o_copy(i).wait_recv()
            y2s[...] = (orecv[1] + orecv[2]) + (orecv[3] + orecv[4])
            y2_copy.start()

    tasks = dict(first=first, pass_on=pass_on, sum_x=sum_x, sum_y=sum_y, activate=activate, gather_x=gather_x,
                 gather_xx=gather_xx, second=second, send_out=send_out, cross=cross)

    def step(s, _):
        for name, lag in ORDER:
            t = s - lag

            @pl.when((t >= (1 if name == "pass_on" else 0)) & (t < CHUNKS))
            def _():
                tasks[name](t)

        return 0

    lax.fori_loop(0, STEPS, step, 0)

    for i in (5, 6, 7):
        o_copy(i).wait_recv()
    y2_copy.wait_recv()
    out_ref[...] = (orecv[0] + orecv[5]) + (orecv[6] + orecv[7]) + y2r[...] + bout_ref[...]

    to_low.wait_send()
    for copy in to_z:
        copy.wait_send()
    for d in (1, 2, 3):
        relay(d).wait_send()
    for t in range(CHUNKS):
        to_sibling(t).wait_send()
        gy_copy(t).wait_send()
        for h in (0, 1):
            gx_copy(t, h).wait_send()
            gxx_copy(t, h).wait_send()
    for t in (CHUNKS - 2, CHUNKS - 1):
        for h in (0, 1):
            x1_copy(t, h).wait_send()
            x2_copy(t, h).wait_send()
        y_copy(t).wait_send()
        c_copy(t).wait_send()
        o_copy(t).wait_send()
    y2_copy.wait_send()


def per_device(tokens, w_in, b_in, w_out, b_out):
    any_space, vmem = pl.BlockSpec(memory_space=pl.ANY), pl.BlockSpec(memory_space=pltpu.VMEM)
    dma = pltpu.SemaphoreType.DMA
    n = CHUNKS
    scratch = [
        pltpu.VMEM((D, FF), BF16), pltpu.VMEM((FF, D), BF16), pltpu.VMEM((n, ROWS, D), BF16),
        pltpu.VMEM((2, 2, ROWS, PAIR), BF16), pltpu.VMEM((n, 2, ROWS, PAIR), BF16), pltpu.VMEM((2, ROWS, PAIR), F32),
        pltpu.VMEM((2, 2, ROWS, QUARTER), BF16), pltpu.VMEM((n, 2, ROWS, QUARTER), BF16), pltpu.VMEM((2, ROWS, QUARTER), F32),
        pltpu.VMEM((2, ROWS, QUARTER), F32), pltpu.VMEM((n, ROWS, QUARTER), F32), pltpu.VMEM((ROWS, QUARTER), F32),
        pltpu.VMEM((n, ROWS, FF), BF16),
        pltpu.VMEM((2, ROWS, D), F32), pltpu.VMEM((n, HALF, D), F32),
        pltpu.VMEM((2, HALF, D), F32), pltpu.VMEM((n, HALF, D), F32),
        pltpu.VMEM((HALF, D), F32), pltpu.VMEM((HALF, D), F32),
        dma((4,)), dma, dma, dma((1,)), dma((n,)), dma((n,)), dma((n,)), dma((4,)), dma((3,)),
        dma((2, 2)), dma((n, 2)), dma((2, 2)), dma((n, 2)), dma((2,)), dma((n,)),
        dma((n,)), dma((n,)), dma((n, 2)), dma((n, 2)), dma((n, 2)), dma((n, 2)),
        dma((2,)), dma((n,)), dma((2,)), dma((n,)), dma, dma,
    ]
    return pl.pallas_call(
        kernel,
        out_shape=jax.ShapeDtypeStruct((HALF, D), F32),
        in_specs=[any_space, any_space, vmem, any_space, vmem],
        out_specs=vmem,
        scratch_shapes=scratch,
        compiler_params=pltpu.CompilerParams(collective_id=0, has_side_effects=True, vmem_limit_bytes=60 * 2**20),
        cost_estimate=pl.CostEstimate(flops=4 * 1024 * D * FF, bytes_accessed=4 * D * FF, transcendentals=1024 * QUARTER),
    )(tokens, w_in, b_in.astype(F32).reshape(1, FF), w_out, b_out.astype(F32).reshape(1, D))


def solution(mesh):
    return jax.shard_map(
        per_device,
        mesh=mesh,
        in_specs=(P("col", "row"), P("row", "col"), P("col"), P("col", "row"), P("row")),
        out_specs=P("col", "row"),
        check_vma=False,
    )
```

time: 399 us -> 149 us (0.37)
  waiting for transfers between devices: 345 us -> 0 us
  Pallas kernels: 0 us -> 144 us
  matrix products: 31.5 us -> 0 us
  between operations: 13.1 us -> 0.01 us
    reduce_scatter x2 -> x0, waiting for transfers between devices: 215 us -> none  [the longest x1 150 us: per_device(): lax.psum_scatter(partial_value, 'row', scatter_dimension=0, tiled=True)]
    pallas_call x0 -> x1, Pallas kernels: none -> 144 us  [per_device(): pl.pallas_call(kernel, out_shape=jax.ShapeDtypeStruct((HALF, D), F32), in...]
    all_gather x2 -> x0, waiting for transfers between devices: 129 us -> none  [the longest x1 87.7 us: per_device(): lax.all_gather(hidden, 'row', axis=0, tiled=True)]
    dot_general x2 -> x0, matrix products: 31.5 us -> none  [the longest x1 16.2 us: per_device(): jnp.dot(lax.all_gather(tokens, 'col', axis=0, tiled=True), w_in, preferre...]
  transfers between devices with their start and end apart: 4 -> 0, of which waited for: 4 -> 0; matrix products, arithmetic and copies ran while one was open for 0% -> 0% of each run, Pallas kernels for 0% -> 0%
where the time goes in v1:
time: 149 us
  Pallas kernels  144 us (97%)
  local copies, waits for them, and re-layouts  3.04 us (2%)
    pallas_call x1, Pallas kernels, per_device(): pl.pallas_call(kernel, out_shape=jax.ShapeDtypeStruct((HALF, D), F32), in...  144 us

profile of v1, /device:TPU:1, one launch (start us, length us, event | category | flops | bytes accessed | tf_op | source)
XLA Modules:
  0.0 148.7 jit_solution(3107629689284243956)
XLA Ops:
  0.0 1.3 reshape.17.bout_ref
  1.3 1.3 reshape.14
  2.6 144.3 %shard_map.55 = f32[64,1536]{1,0:T(8,128)} custom-call(bf16[64,1536]{1,0:T(8,128)(2,1)} %tok_hbm.1, bf16[1536,3072]{1,0:T(8,128)(2,1)} %w1_hbm.1, f32[1,3072]{1,0:T(1,128)} %bitcast.1, bf16[3072,1536]{1,0:T(8,128)(2,1)} %w2_hbm.1, f32[1,1536]{1,0:T(1,128)} %reshape.17.bout_ref), custom_call_target="tpu_custom_call" | custom-call | flops 19327352832 | bytes 18874368 | tf_op jit(solution)/shard_map/pallas_call | solution.py:301
  146.9 1.8 %copy.7 = f32[64,1536]{1,0:T(8,128)} copy(f32[64,1536]{1,0:T(8,128)} %shard_map.55) | data formatting | bytes 786432

commit v2 on v1

--- a/solution.py
+++ b/solution.py
@@ -12,17 +12,35 @@
 D, FF = 1536, 3072
 PAIR, QUARTER = 768, 384
 
+HIDDEN_SCALE, OUT_SCALE = 2.0**20, 2.0**9
+
 ORDER = (
-    ("first", 0), ("pass_on", -1), ("sum_y", 1), ("gather_x", 2), ("second", 3), ("sum_x", 0),
-    ("activate", 1), ("gather_xx", 2), ("send_out", 3), ("cross", 4),
+    ("first", 0), ("pass_on", -1), ("sum_y", 1), ("gather_y", 2), ("second", 3), ("sum_x", 0),
+    ("activate", 1), ("gather_x", 2), ("send_out", 3), ("cross", 4),
 )
 STEPS = CHUNKS + 3
 
 
+def chunk_at(s, lag):
+    t = s - lag
+    return t, (t >= 0) & (t < CHUNKS)
+
+
+def code(v, scale):
+    v = v * scale
+    return ((v * v) * (v * jnp.abs(v))).astype(BF16)
+
+
+def decode(coded, scale):
+    y = coded.astype(F32)
+    r = lax.rsqrt(jnp.maximum(jnp.abs(y), 1e-37))
+    return y * (r * r) * (lax.rsqrt(r) * (1.0 / scale))
+
+
 def kernel(tok_hbm, w1_hbm, bin_ref, w2_hbm, bout_ref, out_ref,
-           w1, w2, tok, x1s, x1r, keep1, x2s, x2r, keep2, ys, yr, keep3, hid, po, cr, osend, orecv, y2s, y2r,
+           w1, w2, tok, x1s, x1r, keep1, ys, yr, keepy, x2s, x2r, keep2, hid, po, cr, osend, orecv, acc, y2s, y2r,
            w1_sem, w2_sem, own_sem, tok_ss, tok_rs, fwd_ss, fwd_rs, first_ss, relay_ss,
-           x1_ss, x1_rs, x2_ss, x2_rs, y_ss, y_rs, gy_ss, gy_rs, gx_ss, gx_rs, gxx_ss, gxx_rs,
+           x1_ss, x1_rs, y_ss, y_rs, x2_ss, x2_rs, gx_ss, gx_rs, gy_ss, gy_rs, gxx_ss, gxx_rs,
            c_ss, c_rs, o_ss, o_rs, y2_ss, y2_rs):
     row, col = lax.axis_index("row"), lax.axis_index("col")
     x, yh = row // 2, row % 2
@@ -43,7 +61,8 @@
     pair_of = tuple(h * 2 * PAIR + mine[h] * PAIR for h in (0, 1))
     other_pair = tuple(h * 2 * PAIR + (1 - mine[h]) * PAIR for h in (0, 1))
     quarter_of = tuple(pair_of[h] + q[h] * QUARTER for h in (0, 1))
-    my_block = quarter_of[0] * (1 - yh) + quarter_of[1] * yh
+    my_half = pl.ds(pl.multiple_of(yh * HALF, HALF), HALF)
+    other_half = pl.ds(pl.multiple_of((1 - yh) * HALF, HALF), HALF)
     dest1, dest2 = (one, three), (three, one)
 
     def cols(start, size):
@@ -123,71 +142,74 @@
 
             part = jnp.dot(tok[t], w1[:, cols(w1_order[i], PAIR)], preferred_element_type=F32)
             if i < 2:
-                x1s[t % 2, h] = part.astype(BF16)
+                x1s[t % 2, h] = code(part, HIDDEN_SCALE)
                 x1_copy(t, h).start()
             else:
                 keep1[h] = part
 
+    def y_copy(t, h):
+        return remote(ys.at[t % 2, h], yr.at[t, h], y_ss.at[t % 2, h], y_rs.at[t, h], across)
+
+    def sum_x(t):
+        for h in (0, 1):
+            x1_copy(t, h).wait_recv()
+
+            @pl.when(t >= 2)
+            def _():
+                y_copy(t, h).wait_send()
+
+            ys[t % 2, h] = code(keep1[h, other_half] + decode(x1r[t, h, other_half], HIDDEN_SCALE), HIDDEN_SCALE)
+            y_copy(t, h).start()
+        for h in (0, 1):
+            keepy[h] = keep1[h, my_half] + decode(x1r[t, h, my_half], HIDDEN_SCALE)
+
     def x2_copy(t, h):
         return remote(x2s.at[t % 2, h], x2r.at[t, h], x2_ss.at[t % 2, h], x2_rs.at[t, h], dest2[h])
 
-    def sum_x(t):
-        for h in (0, 1):
-            x1_copy(t, h).wait_recv()
+    def sum_y(t):
+        for h in (0, 1):
+            y_copy(t, h).wait_recv()
 
             @pl.when(t >= 2)
             def _():
                 x2_copy(t, h).wait_send()
 
             gone = cols((1 - q[h]) * QUARTER, QUARTER)
-            x2s[t % 2, h] = (keep1[h, :, gone] + x1r[t, h, :, gone].astype(F32)).astype(BF16)
+            x2s[t % 2, h] = code(keepy[h, :, gone] + decode(yr[t, h, :, gone], HIDDEN_SCALE), HIDDEN_SCALE)
             x2_copy(t, h).start()
         for h in (0, 1):
             kept = cols(q[h] * QUARTER, QUARTER)
-            keep2[h] = keep1[h, :, kept] + x1r[t, h, :, kept].astype(F32)
-
-    def y_copy(t):
-        return remote(ys.at[t % 2], yr.at[t], y_ss.at[t % 2], y_rs.at[t], across)
-
-    def sum_y(t):
+            keep2[h] = keepy[h, :, kept] + decode(yr[t, h, :, kept], HIDDEN_SCALE)
+
+    def hid_copy(t, rows, start, size, ss, rs, dev):
+        c = cols(start, size)
+        return remote(hid.at[t, rows, c], hid.at[t, rows, c], ss, rs, dev)
+
+    def gx_copy(t, h):
+        return hid_copy(t, my_half, quarter_of[h], QUARTER, gx_ss.at[t, h], gx_rs.at[t, h], dest2[h])
+
+    def gy_copy(t, h):
+        return hid_copy(t, my_half, pair_of[h], PAIR, gy_ss.at[t, h], gy_rs.at[t, h], across)
+
+    def gxx_copy(t, h):
+        return hid_copy(t, pl.ds(0, ROWS), pair_of[h], PAIR, gxx_ss.at[t, h], gxx_rs.at[t, h], dest1[h])
+
+    def activate(t):
         for h in (0, 1):
             x2_copy(t, h).wait_recv()
-
-        @pl.when(t >= 2)
-        def _():
-            y_copy(t).wait_send()
-
-        ys[t % 2] = keep2[1 - yh] + x2r[t, 1 - yh].astype(F32)
-        y_copy(t).start()
-        keep3[...] = keep2[yh] + x2r[t, yh].astype(F32)
-
-    def hid_copy(t, start, size, ss, rs, dev):
-        c = cols(start, size)
-        return remote(hid.at[t, :, c], hid.at[t, :, c], ss, rs, dev)
-
-    def gy_copy(t):
-        return hid_copy(t, my_block, QUARTER, gy_ss.at[t], gy_rs.at[t], across)
-
-    def gx_copy(t, h):
-        return hid_copy(t, quarter_of[h], QUARTER, gx_ss.at[t, h], gx_rs.at[t, h], dest2[h])
-
-    def gxx_copy(t, h):
-        return hid_copy(t, pair_of[h], PAIR, gxx_ss.at[t, h], gxx_rs.at[t, h], dest1[h])
-
-    def activate(t):
-        y_copy(t).wait_recv()
-        c = cols(my_block, QUARTER)
-        hid[t, :, c] = jax.nn.gelu(keep3[...] + yr[t] + bin_ref[:, c], approximate=True).astype(BF16)
-        gy_copy(t).start()
+            c = cols(quarter_of[h], QUARTER)
+            summed = keep2[h] + decode(x2r[t, h], HIDDEN_SCALE)
+            hid[t, my_half, c] = jax.nn.gelu(summed + bin_ref[:, c], approximate=True).astype(BF16)
+            gx_copy(t, h).start()
+
+    def gather_y(t):
+        for h in (0, 1):
+            gx_copy(t, h).wait_recv()
+            gy_copy(t, h).start()
 
     def gather_x(t):
-        gy_copy(t).wait_recv()
-        for h in (0, 1):
-            gx_copy(t, h).start()
-
-    def gather_xx(t):
-        for h in (0, 1):
-            gx_copy(t, h).wait_recv()
+        for h in (0, 1):
+            gy_copy(t, h).wait_recv()
             gxx_copy(t, h).start()
 
     def c_copy(t):
@@ -218,7 +240,7 @@
 
         @pl.when(t < 2)
         def _():
-            orecv[t] = po[t % 2, own_rows] + cr[t]
+            acc[t] = po[t % 2, own_rows] + cr[t]
 
         @pl.when(t >= 2)
         def _():
@@ -226,7 +248,7 @@
             def _():
                 o_copy(t).wait_send()
 
-            osend[t % 2] = po[t % 2, own_rows] + cr[t]
+            osend[t % 2] = code(po[t % 2, own_rows] + cr[t], OUT_SCALE)
             o_copy(t).start()
 
     y2_copy = remote(y2s, y2r, y2_ss, y2_rs, low)
@@ -236,17 +258,17 @@
         def _():
             for i in (2, 3, 4):
                 o_copy(i).wait_recv()
-            y2s[...] = (orecv[1] + orecv[2]) + (orecv[3] + orecv[4])
+            y2s[...] = code(acc[1] + sum(decode(orecv[i], OUT_SCALE) for i in (2, 3, 4)), OUT_SCALE)
             y2_copy.start()
 
-    tasks = dict(first=first, pass_on=pass_on, sum_x=sum_x, sum_y=sum_y, activate=activate, gather_x=gather_x,
-                 gather_xx=gather_xx, second=second, send_out=send_out, cross=cross)
+    tasks = dict(first=first, pass_on=pass_on, sum_x=sum_x, sum_y=sum_y, activate=activate, gather_y=gather_y,
+                 gather_x=gather_x, second=second, send_out=send_out, cross=cross)
 
     def step(s, _):
-        for name, lag in ORDER:
-            t = s - lag
-
-            @pl.when((t >= (1 if name == "pass_on" else 0)) & (t < CHUNKS))
+        for name, *at in ORDER:
+            t, runs = chunk_at(s, *at)
+
+            @pl.when(runs & (t >= (1 if name == "pass_on" else 0)))
             def _():
                 tasks[name](t)
 
@@ -257,7 +279,8 @@
     for i in (5, 6, 7):
         o_copy(i).wait_recv()
     y2_copy.wait_recv()
-    out_ref[...] = (orecv[0] + orecv[5]) + (orecv[6] + orecv[7]) + y2r[...] + bout_ref[...]
+    far = sum(decode(orecv[i], OUT_SCALE) for i in (5, 6, 7))
+    out_ref[...] = acc[0] + far + decode(y2r[...], OUT_SCALE) + bout_ref[...]
 
     to_low.wait_send()
     for copy in to_z:
@@ -266,15 +289,15 @@
         relay(d).wait_send()
     for t in range(CHUNKS):
         to_sibling(t).wait_send()
-        gy_copy(t).wait_send()
         for h in (0, 1):
             gx_copy(t, h).wait_send()
+            gy_copy(t, h).wait_send()
             gxx_copy(t, h).wait_send()
     for t in (CHUNKS - 2, CHUNKS - 1):
         for h in (0, 1):
             x1_copy(t, h).wait_send()
             x2_copy(t, h).wait_send()
-        y_copy(t).wait_send()
+            y_copy(t, h).wait_send()
         c_copy(t).wait_send()
         o_copy(t).wait_send()
     y2_copy.wait_send()
@@ -287,15 +310,14 @@
     scratch = [
         pltpu.VMEM((D, FF), BF16), pltpu.VMEM((FF, D), BF16), pltpu.VMEM((n, ROWS, D), BF16),
         pltpu.VMEM((2, 2, ROWS, PAIR), BF16), pltpu.VMEM((n, 2, ROWS, PAIR), BF16), pltpu.VMEM((2, ROWS, PAIR), F32),
-        pltpu.VMEM((2, 2, ROWS, QUARTER), BF16), pltpu.VMEM((n, 2, ROWS, QUARTER), BF16), pltpu.VMEM((2, ROWS, QUARTER), F32),
-        pltpu.VMEM((2, ROWS, QUARTER), F32), pltpu.VMEM((n, ROWS, QUARTER), F32), pltpu.VMEM((ROWS, QUARTER), F32),
-        pltpu.VMEM((n, ROWS, FF), BF16),
-        pltpu.VMEM((2, ROWS, D), F32), pltpu.VMEM((n, HALF, D), F32),
-        pltpu.VMEM((2, HALF, D), F32), pltpu.VMEM((n, HALF, D), F32),
-        pltpu.VMEM((HALF, D), F32), pltpu.VMEM((HALF, D), F32),
+        pltpu.VMEM((2, 2, HALF, PAIR), BF16), pltpu.VMEM((n, 2, HALF, PAIR), BF16), pltpu.VMEM((2, HALF, PAIR), F32),
+        pltpu.VMEM((2, 2, HALF, QUARTER), BF16), pltpu.VMEM((n, 2, HALF, QUARTER), BF16), pltpu.VMEM((2, HALF, QUARTER), F32),
+        pltpu.VMEM((n, ROWS, FF), BF16), pltpu.VMEM((2, ROWS, D), F32), pltpu.VMEM((n, HALF, D), F32),
+        pltpu.VMEM((2, HALF, D), BF16), pltpu.VMEM((n, HALF, D), BF16), pltpu.VMEM((2, HALF, D), F32),
+        pltpu.VMEM((HALF, D), BF16), pltpu.VMEM((HALF, D), BF16),
         dma((4,)), dma, dma, dma((1,)), dma((n,)), dma((n,)), dma((n,)), dma((4,)), dma((3,)),
-        dma((2, 2)), dma((n, 2)), dma((2, 2)), dma((n, 2)), dma((2,)), dma((n,)),
-        dma((n,)), dma((n,)), dma((n, 2)), dma((n, 2)), dma((n, 2)), dma((n, 2)),
+        dma((2, 2)), dma((n, 2)), dma((2, 2)), dma((n, 2)), dma((2, 2)), dma((n, 2)),
+        dma((n, 2)), dma((n, 2)), dma((n, 2)), dma((n, 2)), dma((n, 2)), dma((n, 2)),
         dma((2,)), dma((n,)), dma((2,)), dma((n,)), dma, dma,
     ]
     return pl.pallas_call(

time: 149 us -> 138 us (0.926)
  Pallas kernels: 144 us -> 132 us
    pallas_call x1, Pallas kernels: 144 us -> 132 us  [per_device(): pl.pallas_call(kernel, out_shape=jax.ShapeDtypeStruct((HALF, D), F32), in...]
where the time goes in v2:
time: 138 us; the launch traced here: 136 us
  Pallas kernels  132 us (96%)
  local copies, waits for them, and re-layouts  3.04 us (2%)
    pallas_call x1, Pallas kernels, per_device(): pl.pallas_call(kernel, out_shape=jax.ShapeDtypeStruct((HALF, D), F32), in...  132 us

profile of v2, /device:TPU:1, one launch (start us, length us, event | category | flops | bytes accessed | tf_op | source)
XLA Modules:
  0.0 136.3 jit_solution(17362752259792158103)
XLA Ops:
  0.0 1.3 reshape.17.bout_ref
  1.3 1.3 reshape.14
  2.6 131.9 %shard_map.55 = f32[64,1536]{1,0:T(8,128)} custom-call(bf16[64,1536]{1,0:T(8,128)(2,1)} %tok_hbm.1, bf16[1536,3072]{1,0:T(8,128)(2,1)} %w1_hbm.1, f32[1,3072]{1,0:T(1,128)} %bitcast.1, bf16[3072,1536]{1,0:T(8,128)(2,1)} %w2_hbm.1, f32[1,1536]{1,0:T(1,128)} %reshape.17.bout_ref), custom_call_target="tpu_custom_call" | custom-call | flops 19327352832 | bytes 18874368 | tf_op jit(solution)/shard_map/pallas_call | solution.py:323
  134.5 1.8 %copy.7 = f32[64,1536]{1,0:T(8,128)} copy(f32[64,1536]{1,0:T(8,128)} %shard_map.55) | data formatting | bytes 786432

commit v3 on v0

v3 whole, which is shorter than its diff:
```python
import jax
import jax.numpy as jnp
from jax import lax
from jax.experimental import pallas as pl
from jax.experimental.pallas import tpu as pltpu
from jax.sharding import PartitionSpec as P

MESH = pl.DeviceIdType.MESH
F32, BF16 = jnp.float32, jnp.bfloat16
GROUPS, SLOTS = 8, 16
ROWS, SLOT, HALF = 128, 64, 32
D, FF = 1536, 3072
PAIR, QUARTER = 768, 384

HIDDEN_SCALE, OUT_SCALE = 2.0**20, 2.0**9

ORDER = (
    ("sum_y0", 3), ("gather_x1", 7), ("first", 0), ("second", 9), ("sum_x1", 2), ("send_out", 10), ("pass_on", -1),
    ("activate1", 4), ("gather_y1", 5), ("sum_y1", 3), ("sum_x0", 1), ("gather_x0", 6), ("gather_y0", 4), ("cross", 12),
    ("activate0", 3),
)
STEPS = 18


def code(v, scale):
    v = v * scale
    return ((v * v) * (v * jnp.abs(v))).astype(BF16)


def decode(coded, scale):
    y = coded.astype(F32)
    r = lax.rsqrt(jnp.maximum(jnp.abs(y), 1e-37))
    return y * (r * r) * (lax.rsqrt(r) * (1.0 / scale))


def kernel(tok_hbm, w1_hbm, bin_ref, w2_hbm, bout_ref, out_ref,
           w1, w2, tok, x1s, x1r, keep, ys, yr, x2s, x2r, hid, po, cr, osend, orecv, acc, y2s, y2r,
           w1_sem, w2_sem, own_sem, first_ss, tok_rs, relay_ss, fwd_ss, fwd_rs,
           x1_ss, x1_rs, y_ss, y_rs, x2_ss, x2_rs, gx_ss, gx_rs, gy_ss, gy_rs, gxx_ss, gxx_rs,
           c_ss, c_rs, o_ss, o_rs, y2_ss, y2_rs):
    row, col = lax.axis_index("row"), lax.axis_index("col")
    x, yh = row // 2, row % 2
    yl, z, core = col // 8, (col // 2) % 4, col % 2
    x_one = x + 1 - 2 * (x % 2)
    x_three = 3 - x
    one = (x_one * 2 + yh, col)
    three = (x_three * 2 + yh, col)
    across = (x * 2 + 1 - yh, col)
    sibling = (row, col + 1 - 2 * core)
    low = (row, (1 - yl) * 8 + z * 2 + core)

    def along_z(d):
        return (row, yl * 8 + ((z + d) % 4) * 2 + core)

    def cols(start, size):
        return pl.ds(pl.multiple_of(start, 128), size)

    def rows(start, size=HALF):
        return pl.ds(pl.multiple_of(start, HALF), size)

    mine = (((x + 1) // 2) % 2, x // 2)
    q = (x // 2, x % 2)
    pair_of = tuple(h * 2 * PAIR + mine[h] * PAIR for h in (0, 1))
    other_pair = tuple(h * 2 * PAIR + (1 - mine[h]) * PAIR for h in (0, 1))
    quarter_of = tuple(pair_of[h] + q[h] * QUARTER for h in (0, 1))
    kept = tuple(cols(q[h] * QUARTER, QUARTER) for h in (0, 1))
    gone = tuple(cols((1 - q[h]) * QUARTER, QUARTER) for h in (0, 1))
    dest1, dest2 = (one, three), (three, one)
    my_half, other_half = rows(yh * HALF), rows((1 - yh) * HALF)
    own_rows, other_rows = rows(core * HALF), rows((1 - core) * HALF)

    def remote(src, dst, ss, rs, dev):
        return pltpu.make_async_remote_copy(src_ref=src, dst_ref=dst, send_sem=ss, recv_sem=rs, device_id=dev, device_id_type=MESH)

    w1_order = (other_pair[0], other_pair[1], pair_of[0], pair_of[1])

    def load_w1(i):
        c = cols(w1_order[i], PAIR)
        return pltpu.make_async_copy(w1_hbm.at[:, c], w1.at[:, c], w1_sem.at[i])

    own = pltpu.make_async_copy(tok_hbm, tok.at[0, :, own_rows], own_sem)
    own.start()
    for i in range(4):
        load_w1(i).start()
    load_w2 = pltpu.make_async_copy(w2_hbm, w2, w2_sem)
    load_w2.start()

    barrier = pltpu.get_barrier_semaphore()
    partners = [one, three, across, sibling, low] + [along_z(d) for d in (1, 2, 3)]
    for dev in partners:
        pl.semaphore_signal(barrier, inc=1, device_id=dev, device_id_type=MESH)
    pl.semaphore_wait(barrier, len(partners))

    def block(r):
        return tok.at[r, :, own_rows]

    def to_sibling(r):
        return remote(block(r), block(r), fwd_ss.at[r], fwd_rs.at[r], sibling)

    def from_sibling(r):
        return remote(tok.at[r, :, other_rows], tok.at[r, :, other_rows], fwd_ss.at[r], fwd_rs.at[r], sibling)

    own.wait()
    to_sibling(0).start()
    to_low = remote(block(0), block(1), first_ss.at[0], tok_rs.at[1], low)
    to_low.start()

    def to_z(d):
        return remote(block(0), block(4 + d), first_ss.at[d], tok_rs.at[4 + d], along_z(4 - d))

    for d in (1, 3, 2):
        to_z(d).start()

    def relay(d):
        return remote(block(1), block(1 + d), relay_ss.at[d - 1], tok_rs.at[1 + d], along_z(4 - d))

    def pass_on(r):
        @pl.when(r >= 1)
        def _():
            remote(block(r), block(r), fwd_ss.at[r], tok_rs.at[r], low).wait_recv()
            to_sibling(r).start()

        @pl.when(r == 1)
        def _():
            for d in (1, 3, 2):
                relay(d).start()

    def x1_copy(k, h):
        return remote(x1s.at[k, h], x1r.at[k, h], x1_ss.at[k, h], x1_rs.at[k, h], dest1[h])

    def first(r):
        from_sibling(r).wait_recv()
        tokens = tok[r].reshape(ROWS, D)
        for i in range(4):
            h = i % 2

            @pl.when(r == 0)
            def _():
                load_w1(i).wait()

            part = jnp.dot(tokens, w1[:, cols(w1_order[i], PAIR)], preferred_element_type=F32)
            for u in (0, 1):
                if i < 2:
                    x1s[2 * r + u, h] = code(part[u * SLOT : (u + 1) * SLOT], HIDDEN_SCALE)
                    x1_copy(2 * r + u, h).start()
                else:
                    keep[2 * r + u, h] = part[u * SLOT : (u + 1) * SLOT]

    def y_copy(k, h):
        return remote(ys.at[k, h], yr.at[k, h], y_ss.at[k, h], y_rs.at[k, h], across)

    def sum_x(k):
        for h in (0, 1):
            x1_copy(k, h).wait_recv()
            ys[k, h] = code(keep[k, h, other_half] + decode(x1r[k, h, other_half], HIDDEN_SCALE), HIDDEN_SCALE)
            y_copy(k, h).start()
        for h in (0, 1):
            keep[k, h, my_half] += decode(x1r[k, h, my_half], HIDDEN_SCALE)

    def x2_copy(k, h):
        return remote(x2s.at[k, h], x2r.at[k, h], x2_ss.at[k, h], x2_rs.at[k, h], dest2[h])

    def sum_y(k):
        for h in (0, 1):
            y_copy(k, h).wait_recv()
            x2s[k, h] = code(keep[k, h, my_half, gone[h]] + decode(yr[k, h, :, gone[h]], HIDDEN_SCALE), HIDDEN_SCALE)
            x2_copy(k, h).start()
        for h in (0, 1):
            keep[k, h, my_half, kept[h]] += decode(yr[k, h, :, kept[h]], HIDDEN_SCALE)

    def hid_copy(k, which, start, size, ss, rs, dev):
        c = cols(start, size)
        return remote(hid.at[k, which, c], hid.at[k, which, c], ss, rs, dev)

    def gx_copy(k, h):
        return hid_copy(k, my_half, quarter_of[h], QUARTER, gx_ss.at[k, h], gx_rs.at[k, h], dest2[h])

    def gy_copy(k, h):
        return hid_copy(k, my_half, pair_of[h], PAIR, gy_ss.at[k, h], gy_rs.at[k, h], across)

    def gxx_copy(k, h):
        return hid_copy(k, pl.ds(0, SLOT), pair_of[h], PAIR, gxx_ss.at[k, h], gxx_rs.at[k, h], dest1[h])

    def activate(k):
        for h in (0, 1):
            x2_copy(k, h).wait_recv()
            c = cols(quarter_of[h], QUARTER)
            summed = keep[k, h, my_half, kept[h]] + decode(x2r[k, h], HIDDEN_SCALE)
            hid[k, my_half, c] = jax.nn.gelu(summed + bin_ref[:, c], approximate=True).astype(BF16)
            gx_copy(k, h).start()

    def gather_y(k):
        for h in (0, 1):
            gx_copy(k, h).wait_recv()
            gy_copy(k, h).start()

    def gather_x(k):
        for h in (0, 1):
            gy_copy(k, h).wait_recv()
            gxx_copy(k, h).start()
        for h in (0, 1):
            x1_copy(k, h).wait_send()
            y_copy(k, h).wait_send()
            x2_copy(k, h).wait_send()

    def c_copy(m):
        r = (m + 1) % GROUPS
        return remote(po.at[m % 2, :, other_rows], cr.at[r], c_ss.at[m % 2], c_rs.at[r], sibling)

    def second(m):
        r = (m + 1) % GROUPS

        @pl.when(m == 0)
        def _():
            load_w2.wait()

        @pl.when(m >= 2)
        def _():
            c_copy(m - 2).wait_send()

        for u in (0, 1):
            for h in (0, 1):
                gxx_copy(2 * r + u, h).wait_recv()
        hidden = hid[pl.ds(2 * r, 2)].reshape(ROWS, FF)
        for i in range(2):
            c = pl.ds(i * PAIR, PAIR)
            po[m % 2, :, :, c] = jnp.dot(hidden, w2[:, c], preferred_element_type=F32).reshape(2, SLOT, PAIR)
        c_copy(m).start()
        for u in (0, 1):
            for h in (0, 1):
                gx_copy(2 * r + u, h).wait_send()
                gy_copy(2 * r + u, h).wait_send()

    def o_copy(m):
        r = (m + 1) % GROUPS
        far = (r + 3) // 4 % 2
        return remote(osend.at[m % 2], orecv.at[r], o_ss.at[m % 2], o_rs.at[r], along_z((r + 3 * far) % 4))

    def send_out(m):
        r = (m + 1) % GROUPS
        c_copy(m).wait_recv()

        @pl.when(r < 2)
        def _():
            acc[r] = po[m % 2, :, own_rows] + cr[r]

        @pl.when(r >= 2)
        def _():
            @pl.when(m >= 3)
            def _():
                o_copy(m - 2).wait_send()

            osend[m % 2] = code(po[m % 2, :, own_rows] + cr[r], OUT_SCALE)
            o_copy(m).start()

        to_sibling(r).wait_send()
        for u in (0, 1):
            for h in (0, 1):
                gxx_copy(2 * r + u, h).wait_send()

    y2_copy = remote(y2s, y2r, y2_ss, y2_rs, low)

    def cross(m):
        @pl.when(m == 3)
        def _():
            for r in (2, 3, 4):
                o_copy(r - 1).wait_recv()
            y2s[...] = code(acc[1] + sum(decode(orecv[r], OUT_SCALE) for r in (2, 3, 4)), OUT_SCALE)
            y2_copy.start()
            to_low.wait_send()
            for d in (1, 2, 3):
                to_z(d).wait_send()
                relay(d).wait_send()

    tasks = dict(first=first, pass_on=pass_on, sum_x=sum_x, sum_y=sum_y, activate=activate, gather_y=gather_y,
                 gather_x=gather_x, second=second, send_out=send_out, cross=cross)

    def step(s, _):
        for name, lag in ORDER:
            p = s - lag

            @pl.when((p >= 0) & (p < GROUPS))
            def _():
                if name[-1] in "01":
                    tasks[name[:-1]]((2 * p + int(name[-1]) + 1) % SLOTS)
                else:
                    tasks[name](p)

        return 0

    lax.fori_loop(0, STEPS, step, 0)

    for r in (5, 6, 7):
        o_copy(r - 1).wait_recv()
    y2_copy.wait_recv()
    far = sum(decode(orecv[r], OUT_SCALE) for r in (5, 6, 7))
    out_ref[...] = acc[0] + far + decode(y2r[...], OUT_SCALE) + bout_ref[...]

    for m in (GROUPS - 2, GROUPS - 1):
        c_copy(m).wait_send()
    for m in (GROUPS - 3, GROUPS - 2):
        o_copy(m).wait_send()
    y2_copy.wait_send()


def per_device(tokens, w_in, b_in, w_out, b_out):
    any_space, vmem = pl.BlockSpec(memory_space=pl.ANY), pl.BlockSpec(memory_space=pltpu.VMEM)
    dma = pltpu.SemaphoreType.DMA
    g, n = GROUPS, SLOTS
    scratch = [
        pltpu.VMEM((D, FF), BF16), pltpu.VMEM((FF, D), BF16), pltpu.VMEM((g, 2, SLOT, D), BF16),
        pltpu.VMEM((n, 2, SLOT, PAIR), BF16), pltpu.VMEM((n, 2, SLOT, PAIR), BF16), pltpu.VMEM((n, 2, SLOT, PAIR), F32),
        pltpu.VMEM((n, 2, HALF, PAIR), BF16), pltpu.VMEM((n, 2, HALF, PAIR), BF16),
        pltpu.VMEM((n, 2, HALF, QUARTER), BF16), pltpu.VMEM((n, 2, HALF, QUARTER), BF16),
        pltpu.VMEM((n, SLOT, FF), BF16), pltpu.VMEM((2, 2, SLOT, D), F32), pltpu.VMEM((g, 2, HALF, D), F32),
        pltpu.VMEM((2, 2, HALF, D), BF16), pltpu.VMEM((g, 2, HALF, D), BF16), pltpu.VMEM((2, 2, HALF, D), F32),
        pltpu.VMEM((2, HALF, D), BF16), pltpu.VMEM((2, HALF, D), BF16),
        dma((4,)), dma, dma, dma((4,)), dma((g,)), dma((3,)), dma((g,)), dma((g,)),
        dma((n, 2)), dma((n, 2)), dma((n, 2)), dma((n, 2)), dma((n, 2)), dma((n, 2)),
        dma((n, 2)), dma((n, 2)), dma((n, 2)), dma((n, 2)), dma((n, 2)), dma((n, 2)),
        dma((2,)), dma((g,)), dma((2,)), dma((g,)), dma, dma,
    ]
    out = pl.pallas_call(
        kernel,
        out_shape=jax.ShapeDtypeStruct((2, HALF, D), F32),
        in_specs=[any_space, any_space, vmem, any_space, vmem],
        out_specs=vmem,
        scratch_shapes=scratch,
        compiler_params=pltpu.CompilerParams(collective_id=0, has_side_effects=True, vmem_limit_bytes=62 * 2**20),
        cost_estimate=pl.CostEstimate(flops=4 * 1024 * D * FF, bytes_accessed=4 * D * FF, transcendentals=1024 * QUARTER),
    )(tokens.reshape(2, HALF, D), w_in, b_in.astype(F32).reshape(1, FF), w_out, b_out.astype(F32).reshape(1, D))
    return out.reshape(2 * HALF, D)


def solution(mesh):
    return jax.shard_map(
        per_device,
        mesh=mesh,
        in_specs=(P("col", "row"), P("row", "col"), P("col"), P("col", "row"), P("row")),
        out_specs=P("col", "row"),
        check_vma=False,
    )
```

time: 399 us -> 123 us (0.31)
  waiting for transfers between devices: 345 us -> 0 us
  Pallas kernels: 0 us -> 118 us
  matrix products: 31.5 us -> 0 us
  between operations: 13.1 us -> 0.01 us
    reduce_scatter x2 -> x0, waiting for transfers between devices: 215 us -> none  [the longest x1 150 us: per_device(): lax.psum_scatter(partial_value, 'row', scatter_dimension=0, tiled=True)]
    all_gather x2 -> x0, waiting for transfers between devices: 129 us -> none  [the longest x1 87.7 us: per_device(): lax.all_gather(hidden, 'row', axis=0, tiled=True)]
    pallas_call x0 -> x1, Pallas kernels: none -> 118 us  [per_device(): pl.pallas_call(kernel, out_shape=jax.ShapeDtypeStruct((2, HALF, D), F32),...]
    dot_general x2 -> x0, matrix products: 31.5 us -> none  [the longest x1 16.2 us: per_device(): jnp.dot(lax.all_gather(tokens, 'col', axis=0, tiled=True), w_in, preferre...]
  transfers between devices with their start and end apart: 4 -> 0, of which waited for: 4 -> 0; matrix products, arithmetic and copies ran while one was open for 0% -> 0% of each run, Pallas kernels for 0% -> 0%
where the time goes in v3:
time: 123 us
  Pallas kernels  118 us (96%)
  local copies, waits for them, and re-layouts  3.04 us (2%)
  other arithmetic  1.29 us (1%)
    pallas_call x1, Pallas kernels, per_device(): pl.pallas_call(kernel, out_shape=jax.ShapeDtypeStruct((2, HALF, D), F32),...  118 us

profile of v3, /device:TPU:1, one launch (start us, length us, event | category | flops | bytes accessed | tf_op | source)
XLA Modules:
  0.0 122.5 jit_solution(7205612275220073298)
XLA Ops:
  0.0 1.3 %reshape.25.bout_ref = f32[1,1536]{1,0:T(1,128)} reshape(bf16[1536]{0:T(1024)(128)(2,1)} %param.9) | data formatting | bytes 9216 | tf_op jit(solution)/shard_map/reshape | solution.py:331
  1.3 1.3 %reshape.22 = f32[3072]{0:T(1024)} convert(bf16[3072]{0:T(1024)(128)(2,1)} %param.7) | non-fusion elementwise | flops 3072 | bytes 18432 | tf_op jit(solution)/shard_map/reshape | solution.py:331
  2.6 118.2 %shard_map.55 = f32[2,32,1536]{2,1,0:T(8,128)} custom-call(bf16[2,32,1536]{2,1,0:T(8,128)(2,1)} %bitcast.5, bf16[1536,3072]{1,0:T(8,128)(2,1)} %w1_hbm.1, f32[1,3072]{1,0:T(1,128)} %bitcast.4, bf16[3072,1536]{1,0:T(8,128)(2,1)} %w2_hbm.1, f32[1,1536]{1,0:T(1,128)} %reshape.25.bout_ref), custom_call_target="tpu_custom_call" | custom-call | flops 19327352832 | bytes 18874368 | tf_op jit(solution)/shard_map/pallas_call | solution.py:323
  120.8 1.8 %copy.7 = f32[64,1536]{1,0:T(8,128)} copy(f32[64,1536]{1,0:T(8,128)} %bitcast.3) | data formatting | bytes 786432

commit v4 on v3

--- a/solution.py
+++ b/solution.py
@@ -15,11 +15,11 @@
 HIDDEN_SCALE, OUT_SCALE = 2.0**20, 2.0**9
 
 ORDER = (
-    ("sum_y0", 3), ("gather_x1", 7), ("first", 0), ("second", 9), ("sum_x1", 2), ("send_out", 10), ("pass_on", -1),
-    ("activate1", 4), ("gather_y1", 5), ("sum_y1", 3), ("sum_x0", 1), ("gather_x0", 6), ("gather_y0", 4), ("cross", 12),
-    ("activate0", 3),
+    ("first", 0), ("sum_x1", 1), ("gather_y0", 5), ("second", 9), ("activate1", 3), ("sum_y1", 2), ("activate0", 2),
+    ("gather_x1", 7), ("cross", 11), ("sum_y0", 1), ("sum_x0", 0), ("pass_on", -1), ("send_out", 9), ("gather_x0", 6),
+    ("gather_y1", 5),
 )
-STEPS = 18
+STEPS = 17
 
 
 def code(v, scale):
@@ -33,8 +33,8 @@
     return y * (r * r) * (lax.rsqrt(r) * (1.0 / scale))
 
 
-def kernel(tok_hbm, w1_hbm, bin_ref, w2_hbm, bout_ref, out_ref,
-           w1, w2, tok, x1s, x1r, keep, ys, yr, x2s, x2r, hid, po, cr, osend, orecv, acc, y2s, y2r,
+def kernel(tok_hbm, w1_hbm, bin_ref, w2_hbm, out_ref,
+           w1, w2, bias, tok, x1s, x1r, keep, ys, yr, x2s, x2r, hid, po, cr, osend, orecv, acc, y2s, y2r,
            w1_sem, w2_sem, own_sem, first_ss, tok_rs, relay_ss, fwd_ss, fwd_rs,
            x1_ss, x1_rs, y_ss, y_rs, x2_ss, x2_rs, gx_ss, gx_rs, gy_ss, gy_rs, gxx_ss, gxx_rs,
            c_ss, c_rs, o_ss, o_rs, y2_ss, y2_rs):
@@ -83,14 +83,16 @@
     for i in range(4):
         load_w1(i).start()
     load_w2 = pltpu.make_async_copy(w2_hbm, w2, w2_sem)
-    load_w2.start()
-
+
+    bias[...] = bin_ref[...].astype(F32).reshape(1, FF)
     barrier = pltpu.get_barrier_semaphore()
     partners = [one, three, across, sibling, low] + [along_z(d) for d in (1, 2, 3)]
     for dev in partners:
         pl.semaphore_signal(barrier, inc=1, device_id=dev, device_id_type=MESH)
     pl.semaphore_wait(barrier, len(partners))
 
+    near = {1: 1, 2: 6, 3: 7}
+
     def block(r):
         return tok.at[r, :, own_rows]
 
@@ -102,28 +104,34 @@
 
     own.wait()
     to_sibling(0).start()
-    to_low = remote(block(0), block(1), first_ss.at[0], tok_rs.at[1], low)
+    to_low = remote(block(0), block(2), first_ss.at[0], tok_rs.at[2], low)
     to_low.start()
 
     def to_z(d):
-        return remote(block(0), block(4 + d), first_ss.at[d], tok_rs.at[4 + d], along_z(4 - d))
-
-    for d in (1, 3, 2):
-        to_z(d).start()
+        return remote(block(0), block(near[d]), first_ss.at[d], tok_rs.at[near[d]], along_z(4 - d))
+
+    to_z(1).start()
 
     def relay(d):
-        return remote(block(1), block(1 + d), relay_ss.at[d - 1], tok_rs.at[1 + d], along_z(4 - d))
-
-    def pass_on(r):
-        @pl.when(r >= 1)
-        def _():
-            remote(block(r), block(r), fwd_ss.at[r], tok_rs.at[r], low).wait_recv()
-            to_sibling(r).start()
-
-        @pl.when(r == 1)
-        def _():
+        return remote(block(2), block(2 + d), relay_ss.at[d - 1], tok_rs.at[2 + d], along_z(4 - d))
+
+    def take(r):
+        remote(block(r), block(r), fwd_ss.at[r], tok_rs.at[r], low).wait_recv()
+        to_sibling(r).start()
+
+    def pass_on(p):
+        @pl.when(p == 1)
+        def _():
+            take(1)
+            take(2)
             for d in (1, 3, 2):
                 relay(d).start()
+            for d in (3, 2):
+                to_z(d).start()
+
+        @pl.when((p > 1) & (p < GROUPS - 1))
+        def _():
+            take(p + 1)
 
     def x1_copy(k, h):
         return remote(x1s.at[k, h], x1r.at[k, h], x1_ss.at[k, h], x1_rs.at[k, h], dest1[h])
@@ -131,6 +139,11 @@
     def first(r):
         from_sibling(r).wait_recv()
         tokens = tok[r].reshape(ROWS, D)
+
+        @pl.when(r == 1)
+        def _():
+            load_w2.start()
+
         for i in range(4):
             h = i % 2
 
@@ -186,7 +199,7 @@
             x2_copy(k, h).wait_recv()
             c = cols(quarter_of[h], QUARTER)
             summed = keep[k, h, my_half, kept[h]] + decode(x2r[k, h], HIDDEN_SCALE)
-            hid[k, my_half, c] = jax.nn.gelu(summed + bin_ref[:, c], approximate=True).astype(BF16)
+            hid[k, my_half, c] = jax.nn.gelu(summed + bias[:, c], approximate=True).astype(BF16)
             gx_copy(k, h).start()
 
     def gather_y(k):
@@ -233,20 +246,24 @@
 
     def o_copy(m):
         r = (m + 1) % GROUPS
-        far = (r + 3) // 4 % 2
-        return remote(osend.at[m % 2], orecv.at[r], o_ss.at[m % 2], o_rs.at[r], along_z((r + 3 * far) % 4))
+        far = (r + 2) // 4 % 2
+        return remote(osend.at[m % 2], orecv.at[r], o_ss.at[m % 2], o_rs.at[r], along_z((r + 2 * far) % 4))
 
     def send_out(m):
         r = (m + 1) % GROUPS
         c_copy(m).wait_recv()
 
-        @pl.when(r < 2)
-        def _():
-            acc[r] = po[m % 2, :, own_rows] + cr[r]
-
-        @pl.when(r >= 2)
-        def _():
-            @pl.when(m >= 3)
+        @pl.when((m == 1) | (m == 7))
+        def _():
+            acc[m // 4] = po[m % 2, :, own_rows] + cr[r]
+
+        @pl.when((m != 1) & (m != 7))
+        def _():
+            @pl.when(m == 2)
+            def _():
+                o_copy(0).wait_send()
+
+            @pl.when(m >= 4)
             def _():
                 o_copy(m - 2).wait_send()
 
@@ -261,11 +278,11 @@
     y2_copy = remote(y2s, y2r, y2_ss, y2_rs, low)
 
     def cross(m):
-        @pl.when(m == 3)
-        def _():
-            for r in (2, 3, 4):
+        @pl.when(m == 4)
+        def _():
+            for r in (3, 4, 5):
                 o_copy(r - 1).wait_recv()
-            y2s[...] = code(acc[1] + sum(decode(orecv[r], OUT_SCALE) for r in (2, 3, 4)), OUT_SCALE)
+            y2s[...] = code(acc[0] + sum(decode(orecv[r], OUT_SCALE) for r in (3, 4, 5)), OUT_SCALE)
             y2_copy.start()
             to_low.wait_send()
             for d in (1, 2, 3):
@@ -282,7 +299,8 @@
             @pl.when((p >= 0) & (p < GROUPS))
             def _():
                 if name[-1] in "01":
-                    tasks[name[:-1]]((2 * p + int(name[-1]) + 1) % SLOTS)
+                    r = (p + 1) % GROUPS if name.startswith("gather") else p
+                    tasks[name[:-1]](2 * r + int(name[-1]))
                 else:
                     tasks[name](p)
 
@@ -290,15 +308,15 @@
 
     lax.fori_loop(0, STEPS, step, 0)
 
-    for r in (5, 6, 7):
+    for r in (1, 6, 7):
         o_copy(r - 1).wait_recv()
     y2_copy.wait_recv()
-    far = sum(decode(orecv[r], OUT_SCALE) for r in (5, 6, 7))
-    out_ref[...] = acc[0] + far + decode(y2r[...], OUT_SCALE) + bout_ref[...]
+    far = sum(decode(orecv[r], OUT_SCALE) for r in (1, 6, 7))
+    out_ref[...] = acc[1] + far + decode(y2r[...], OUT_SCALE)
 
     for m in (GROUPS - 2, GROUPS - 1):
         c_copy(m).wait_send()
-    for m in (GROUPS - 3, GROUPS - 2):
+    for m in (5, 6):
         o_copy(m).wait_send()
     y2_copy.wait_send()
 
@@ -308,7 +326,7 @@
     dma = pltpu.SemaphoreType.DMA
     g, n = GROUPS, SLOTS
     scratch = [
-        pltpu.VMEM((D, FF), BF16), pltpu.VMEM((FF, D), BF16), pltpu.VMEM((g, 2, SLOT, D), BF16),
+        pltpu.VMEM((D, FF), BF16), pltpu.VMEM((FF, D), BF16), pltpu.VMEM((1, FF), F32), pltpu.VMEM((g, 2, SLOT, D), BF16),
         pltpu.VMEM((n, 2, SLOT, PAIR), BF16), pltpu.VMEM((n, 2, SLOT, PAIR), BF16), pltpu.VMEM((n, 2, SLOT, PAIR), F32),
         pltpu.VMEM((n, 2, HALF, PAIR), BF16), pltpu.VMEM((n, 2, HALF, PAIR), BF16),
         pltpu.VMEM((n, 2, HALF, QUARTER), BF16), pltpu.VMEM((n, 2, HALF, QUARTER), BF16),
@@ -323,13 +341,13 @@
     out = pl.pallas_call(
         kernel,
         out_shape=jax.ShapeDtypeStruct((2, HALF, D), F32),
-        in_specs=[any_space, any_space, vmem, any_space, vmem],
+        in_specs=[any_space, any_space, vmem, any_space],
         out_specs=vmem,
         scratch_shapes=scratch,
         compiler_params=pltpu.CompilerParams(collective_id=0, has_side_effects=True, vmem_limit_bytes=62 * 2**20),
         cost_estimate=pl.CostEstimate(flops=4 * 1024 * D * FF, bytes_accessed=4 * D * FF, transcendentals=1024 * QUARTER),
-    )(tokens.reshape(2, HALF, D), w_in, b_in.astype(F32).reshape(1, FF), w_out, b_out.astype(F32).reshape(1, D))
-    return out.reshape(2 * HALF, D)
+    )(tokens.reshape(2, HALF, D), w_in, b_in, w_out)
+    return out.reshape(2 * HALF, D) + b_out.astype(F32)
 
 
 def solution(mesh):

time: 123 us -> 116 us (0.943); the launches traced: 123 us -> 114 us
  Pallas kernels: 118 us -> 112 us
  local copies, waits for them, and re-layouts: 3.04 us -> 0 us
    pallas_call x1, Pallas kernels: 118 us -> 112 us  [per_device(): pl.pallas_call(kernel, out_shape=jax.ShapeDtypeStruct((2, HALF, D), F32),...]
    add x0 -> x1, other arithmetic: none -> 1.77 us  [per_device(): return out.reshape(2 * HALF, D) + b_out.astype(F32)]
    unnamed x1 -> x0, local copies, waits for them, and re-layouts: 1.77 us -> none
    reshape x1 -> x0, other arithmetic: 1.29 us -> none  [per_device(): b_in.astype(F32).reshape(1, FF)]
    reshape x1 -> x0, local copies, waits for them, and re-layouts: 1.27 us -> none  [per_device(): b_out.astype(F32).reshape(1, D)]
where the time goes in v4:
time: 116 us; the launch traced here: 114 us
  Pallas kernels  112 us (97%)
  other arithmetic  2.46 us (2%)
    pallas_call x1, Pallas kernels, per_device(): pl.pallas_call(kernel, out_shape=jax.ShapeDtypeStruct((2, HALF, D), F32),...  112 us

profile of v4, /device:TPU:1, one launch (start us, length us, event | category | flops | bytes accessed | tf_op | source)
XLA Modules:
  0.0 114.2 jit_solution(3259571895886154608)
XLA Ops:
  0.0 0.7 convert_element_type.3
  0.7 111.7 %shard_map.55 = f32[2,32,1536]{2,1,0:T(8,128)} custom-call(bf16[2,32,1536]{2,1,0:T(8,128)(2,1)} %bitcast.3, bf16[1536,3072]{1,0:T(8,128)(2,1)} %w1_hbm.1, bf16[3072]{0:T(1024)(128)(2,1)} %bin_ref.1, bf16[3072,1536]{1,0:T(8,128)(2,1)} %w2_hbm.1), custom_call_target="tpu_custom_call" | custom-call | flops 19327352832 | bytes 18874368 | tf_op jit(solution)/shard_map/pallas_call | solution.py:341
  112.4 1.8 %bitcast_add_fusion = f32[64,1536]{1,0:T(8,128)} fusion(f32[2,32,1536]{2,1,0:T(8,128)} %shard_map.55, f32[1536]{0:T(1024)S(1)} %convert_element_type.3), kind=kLoop, calls=%fused_computation | loop fusion | flops 98304 | bytes 792576 | tf_op jit(solution)/shard_map/add | solution.py:350

commit v5 on v4

--- a/solution.py
+++ b/solution.py
@@ -33,9 +33,9 @@
     return y * (r * r) * (lax.rsqrt(r) * (1.0 / scale))
 
 
-def kernel(tok_hbm, w1_hbm, bin_ref, w2_hbm, out_ref,
-           w1, w2, bias, tok, x1s, x1r, keep, ys, yr, x2s, x2r, hid, po, cr, osend, orecv, acc, y2s, y2r,
-           w1_sem, w2_sem, own_sem, first_ss, tok_rs, relay_ss, fwd_ss, fwd_rs,
+def kernel(tok_hbm, w1_hbm, bin_hbm, w2_hbm, bout_hbm, out_ref,
+           w1, w2, bin_raw, bout_raw, bias_in, bias_out, tok, x1s, x1r, keep, ys, yr, x2s, x2r, hid, po, cr, osend, orecv, acc, y2s, y2r,
+           w1_sem, w2_sem, bias_sem, own_sem, first_ss, tok_rs, relay_ss, fwd_ss, fwd_rs,
            x1_ss, x1_rs, y_ss, y_rs, x2_ss, x2_rs, gx_ss, gx_rs, gy_ss, gy_rs, gxx_ss, gxx_rs,
            c_ss, c_rs, o_ss, o_rs, y2_ss, y2_rs):
     row, col = lax.axis_index("row"), lax.axis_index("col")
@@ -72,6 +72,11 @@
     def remote(src, dst, ss, rs, dev):
         return pltpu.make_async_remote_copy(src_ref=src, dst_ref=dst, send_sem=ss, recv_sem=rs, device_id=dev, device_id_type=MESH)
 
+    barrier = pltpu.get_barrier_semaphore()
+    partners = [one, three, across, sibling, low] + [along_z(d) for d in (1, 2, 3)]
+    for dev in partners:
+        pl.semaphore_signal(barrier, inc=1, device_id=dev, device_id_type=MESH)
+
     w1_order = (other_pair[0], other_pair[1], pair_of[0], pair_of[1])
 
     def load_w1(i):
@@ -82,13 +87,12 @@
     own.start()
     for i in range(4):
         load_w1(i).start()
+    load_bin = pltpu.make_async_copy(bin_hbm, bin_raw, bias_sem.at[0])
+    load_bin.start()
+    load_bout = pltpu.make_async_copy(bout_hbm, bout_raw, bias_sem.at[1])
+    load_bout.start()
     load_w2 = pltpu.make_async_copy(w2_hbm, w2, w2_sem)
 
-    bias[...] = bin_ref[...].astype(F32).reshape(1, FF)
-    barrier = pltpu.get_barrier_semaphore()
-    partners = [one, three, across, sibling, low] + [along_z(d) for d in (1, 2, 3)]
-    for dev in partners:
-        pl.semaphore_signal(barrier, inc=1, device_id=dev, device_id_type=MESH)
     pl.semaphore_wait(barrier, len(partners))
 
     near = {1: 1, 2: 6, 3: 7}
@@ -143,6 +147,10 @@
         @pl.when(r == 1)
         def _():
             load_w2.start()
+            load_bin.wait()
+            load_bout.wait()
+            bias_in[...] = bin_raw[...].astype(F32).reshape(1, FF)
+            bias_out[...] = bout_raw[...].astype(F32).reshape(1, D)
 
         for i in range(4):
             h = i % 2
@@ -199,7 +207,7 @@
             x2_copy(k, h).wait_recv()
             c = cols(quarter_of[h], QUARTER)
             summed = keep[k, h, my_half, kept[h]] + decode(x2r[k, h], HIDDEN_SCALE)
-            hid[k, my_half, c] = jax.nn.gelu(summed + bias[:, c], approximate=True).astype(BF16)
+            hid[k, my_half, c] = jax.nn.gelu(summed + bias_in[:, c], approximate=True).astype(BF16)
             gx_copy(k, h).start()
 
     def gather_y(k):
@@ -216,9 +224,9 @@
             y_copy(k, h).wait_send()
             x2_copy(k, h).wait_send()
 
-    def c_copy(m):
-        r = (m + 1) % GROUPS
-        return remote(po.at[m % 2, :, other_rows], cr.at[r], c_ss.at[m % 2], c_rs.at[r], sibling)
+    def c_copy(m, i):
+        r, c = (m + 1) % GROUPS, pl.ds(i * PAIR, PAIR)
+        return remote(po.at[m % 2, :, other_rows, c], cr.at[r, :, :, c], c_ss.at[m % 2, i], c_rs.at[r, i], sibling)
 
     def second(m):
         r = (m + 1) % GROUPS
@@ -229,46 +237,49 @@
 
         @pl.when(m >= 2)
         def _():
-            c_copy(m - 2).wait_send()
+            for i in (0, 1):
+                c_copy(m - 2, i).wait_send()
 
         for u in (0, 1):
             for h in (0, 1):
                 gxx_copy(2 * r + u, h).wait_recv()
         hidden = hid[pl.ds(2 * r, 2)].reshape(ROWS, FF)
-        for i in range(2):
+        for i in (0, 1):
             c = pl.ds(i * PAIR, PAIR)
             po[m % 2, :, :, c] = jnp.dot(hidden, w2[:, c], preferred_element_type=F32).reshape(2, SLOT, PAIR)
-        c_copy(m).start()
+            c_copy(m, i).start()
         for u in (0, 1):
             for h in (0, 1):
                 gx_copy(2 * r + u, h).wait_send()
                 gy_copy(2 * r + u, h).wait_send()
 
-    def o_copy(m):
-        r = (m + 1) % GROUPS
+    def o_copy(m, i):
+        r, c = (m + 1) % GROUPS, pl.ds(i * PAIR, PAIR)
         far = (r + 2) // 4 % 2
-        return remote(osend.at[m % 2], orecv.at[r], o_ss.at[m % 2], o_rs.at[r], along_z((r + 2 * far) % 4))
+        return remote(osend.at[m % 2, :, :, c], orecv.at[r, :, :, c], o_ss.at[m % 2, i], o_rs.at[r, i], along_z((r + 2 * far) % 4))
 
     def send_out(m):
         r = (m + 1) % GROUPS
-        c_copy(m).wait_recv()
-
-        @pl.when((m == 1) | (m == 7))
-        def _():
-            acc[m // 4] = po[m % 2, :, own_rows] + cr[r]
-
-        @pl.when((m != 1) & (m != 7))
-        def _():
-            @pl.when(m == 2)
+        for i in (0, 1):
+            c = pl.ds(i * PAIR, PAIR)
+            c_copy(m, i).wait_recv()
+
+            @pl.when((m == 1) | (m == 7))
             def _():
-                o_copy(0).wait_send()
-
-            @pl.when(m >= 4)
+                acc[m // 4, :, :, c] = po[m % 2, :, own_rows, c] + cr[r, :, :, c]
+
+            @pl.when((m != 1) & (m != 7))
             def _():
-                o_copy(m - 2).wait_send()
-
-            osend[m % 2] = code(po[m % 2, :, own_rows] + cr[r], OUT_SCALE)
-            o_copy(m).start()
+                @pl.when(m == 2)
+                def _():
+                    o_copy(0, i).wait_send()
+
+                @pl.when(m >= 4)
+                def _():
+                    o_copy(m - 2, i).wait_send()
+
+                osend[m % 2, :, :, c] = code(po[m % 2, :, own_rows, c] + cr[r, :, :, c], OUT_SCALE)
+                o_copy(m, i).start()
 
         to_sibling(r).wait_send()
         for u in (0, 1):
@@ -281,7 +292,8 @@
         @pl.when(m == 4)
         def _():
             for r in (3, 4, 5):
-                o_copy(r - 1).wait_recv()
+                for i in (0, 1):
+                    o_copy(r - 1, i).wait_recv()
             y2s[...] = code(acc[0] + sum(decode(orecv[r], OUT_SCALE) for r in (3, 4, 5)), OUT_SCALE)
             y2_copy.start()
             to_low.wait_send()
@@ -309,15 +321,17 @@
     lax.fori_loop(0, STEPS, step, 0)
 
     for r in (1, 6, 7):
-        o_copy(r - 1).wait_recv()
+        for i in (0, 1):
+            o_copy(r - 1, i).wait_recv()
     y2_copy.wait_recv()
     far = sum(decode(orecv[r], OUT_SCALE) for r in (1, 6, 7))
-    out_ref[...] = acc[1] + far + decode(y2r[...], OUT_SCALE)
-
-    for m in (GROUPS - 2, GROUPS - 1):
-        c_copy(m).wait_send()
-    for m in (5, 6):
-        o_copy(m).wait_send()
+    out_ref[...] = acc[1] + far + decode(y2r[...], OUT_SCALE) + bias_out[...]
+
+    for i in (0, 1):
+        for m in (GROUPS - 2, GROUPS - 1):
+            c_copy(m, i).wait_send()
+        for m in (5, 6):
+            o_copy(m, i).wait_send()
     y2_copy.wait_send()
 
 
@@ -326,28 +340,28 @@
     dma = pltpu.SemaphoreType.DMA
     g, n = GROUPS, SLOTS
     scratch = [
-        pltpu.VMEM((D, FF), BF16), pltpu.VMEM((FF, D), BF16), pltpu.VMEM((1, FF), F32), pltpu.VMEM((g, 2, SLOT, D), BF16),
+        pltpu.VMEM((D, FF), BF16), pltpu.VMEM((FF, D), BF16), pltpu.VMEM((FF,), BF16), pltpu.VMEM((D,), BF16), pltpu.VMEM((1, FF), F32), pltpu.VMEM((1, D), F32), pltpu.VMEM((g, 2, SLOT, D), BF16),
         pltpu.VMEM((n, 2, SLOT, PAIR), BF16), pltpu.VMEM((n, 2, SLOT, PAIR), BF16), pltpu.VMEM((n, 2, SLOT, PAIR), F32),
         pltpu.VMEM((n, 2, HALF, PAIR), BF16), pltpu.VMEM((n, 2, HALF, PAIR), BF16),
         pltpu.VMEM((n, 2, HALF, QUARTER), BF16), pltpu.VMEM((n, 2, HALF, QUARTER), BF16),
         pltpu.VMEM((n, SLOT, FF), BF16), pltpu.VMEM((2, 2, SLOT, D), F32), pltpu.VMEM((g, 2, HALF, D), F32),
         pltpu.VMEM((2, 2, HALF, D), BF16), pltpu.VMEM((g, 2, HALF, D), BF16), pltpu.VMEM((2, 2, HALF, D), F32),
         pltpu.VMEM((2, HALF, D), BF16), pltpu.VMEM((2, HALF, D), BF16),
-        dma((4,)), dma, dma, dma((4,)), dma((g,)), dma((3,)), dma((g,)), dma((g,)),
+        dma((4,)), dma, dma((2,)), dma, dma((4,)), dma((g,)), dma((3,)), dma((g,)), dma((g,)),
         dma((n, 2)), dma((n, 2)), dma((n, 2)), dma((n, 2)), dma((n, 2)), dma((n, 2)),
         dma((n, 2)), dma((n, 2)), dma((n, 2)), dma((n, 2)), dma((n, 2)), dma((n, 2)),
-        dma((2,)), dma((g,)), dma((2,)), dma((g,)), dma, dma,
+        dma((2, 2)), dma((g, 2)), dma((2, 2)), dma((g, 2)), dma, dma,
     ]
     out = pl.pallas_call(
         kernel,
-        out_shape=jax.ShapeDtypeStruct((2, HALF, D), F32),
-        in_specs=[any_space, any_space, vmem, any_space],
+        out_shape=pltpu.VMEM((2, HALF, D), F32),
+        in_specs=[any_space] * 5,
         out_specs=vmem,
         scratch_shapes=scratch,
         compiler_params=pltpu.CompilerParams(collective_id=0, has_side_effects=True, vmem_limit_bytes=62 * 2**20),
         cost_estimate=pl.CostEstimate(flops=4 * 1024 * D * FF, bytes_accessed=4 * D * FF, transcendentals=1024 * QUARTER),
-    )(tokens.reshape(2, HALF, D), w_in, b_in, w_out)
-    return out.reshape(2 * HALF, D) + b_out.astype(F32)
+    )(tokens.reshape(2, HALF, D), w_in, b_in, w_out, b_out)
+    return out.reshape(2 * HALF, D)
 
 
 def solution(mesh):

time: 116 us -> 113 us (0.974)
  other arithmetic: 2.46 us -> 0 us
    add x1 -> x0, other arithmetic: 1.77 us -> none  [per_device(): return out.reshape(2 * HALF, D) + b_out.astype(F32)]
where the time goes in v5:
time: 113 us; the launch traced here: 111 us
  Pallas kernels  111 us (98%)
    pallas_call x1, Pallas kernels, per_device(): pl.pallas_call(kernel, out_shape=pltpu.VMEM((2, HALF, D), F32), in_specs=...  111 us

profile of v5, /device:TPU:1, one launch (start us, length us, event | category | flops | bytes accessed | tf_op | source)
XLA Modules:
  0.0 111.3 jit_solution(6027324155260187733)
XLA Ops:
  0.0 110.6 %shard_map.55 = f32[2,32,1536]{2,1,0:T(8,128)S(1)} custom-call(bf16[2,32,1536]{2,1,0:T(8,128)(2,1)} %bitcast.3, bf16[1536,3072]{1,0:T(8,128)(2,1)} %w1_hbm.1, bf16[3072]{0:T(1024)(128)(2,1)} %bin_hbm.1, bf16[3072,1536]{1,0:T(8,128)(2,1)} %w2_hbm.1, bf16[1536]{0:T(1024)(128)(2,1)} %bout_hbm.1), custom_call_target="tpu_custom_call" | custom-call | flops 19327352832 | bytes 18874368 | tf_op jit(solution)/shard_map/pallas_call | solution.py:355
  110.6 0.7 copy.7

commit v6 on v5

--- a/solution.py
+++ b/solution.py
@@ -15,11 +15,11 @@
 HIDDEN_SCALE, OUT_SCALE = 2.0**20, 2.0**9
 
 ORDER = (
-    ("first", 0), ("sum_x1", 1), ("gather_y0", 5), ("second", 9), ("activate1", 3), ("sum_y1", 2), ("activate0", 2),
-    ("gather_x1", 7), ("cross", 11), ("sum_y0", 1), ("sum_x0", 0), ("pass_on", -1), ("send_out", 9), ("gather_x0", 6),
-    ("gather_y1", 5),
+    ("send_out", 12), ("pass_on", 0), ("first", 0), ("second", 11), ("activate0", 4), ("sum_x0", 1), ("activate1", 4),
+    ("gather_x0", 9), ("sum_y0", 2), ("sum_x1", 1), ("cross", 13), ("gather_x1", 8), ("gather_y0", 7), ("sum_y1", 2),
+    ("gather_y1", 6),
 )
-STEPS = 17
+STEPS = 20
 
 
 def code(v, scale):
@@ -35,7 +35,7 @@
 
 def kernel(tok_hbm, w1_hbm, bin_hbm, w2_hbm, bout_hbm, out_ref,
            w1, w2, bin_raw, bout_raw, bias_in, bias_out, tok, x1s, x1r, keep, ys, yr, x2s, x2r, hid, po, cr, osend, orecv, acc, y2s, y2r,
-           w1_sem, w2_sem, bias_sem, own_sem, first_ss, tok_rs, relay_ss, fwd_ss, fwd_rs,
+           w1_sem, w2_sem, bias_sem, own_sem, first_ss, tok_rs, z_ss, fwd_ss, fwd_rs,
            x1_ss, x1_rs, y_ss, y_rs, x2_ss, x2_rs, gx_ss, gx_rs, gy_ss, gy_rs, gxx_ss, gxx_rs,
            c_ss, c_rs, o_ss, o_rs, y2_ss, y2_rs):
     row, col = lax.axis_index("row"), lax.axis_index("col")
@@ -95,8 +95,6 @@
 
     pl.semaphore_wait(barrier, len(partners))
 
-    near = {1: 1, 2: 6, 3: 7}
-
     def block(r):
         return tok.at[r, :, own_rows]
 
@@ -108,16 +106,19 @@
 
     own.wait()
     to_sibling(0).start()
-    to_low = remote(block(0), block(2), first_ss.at[0], tok_rs.at[2], low)
+    to_low = remote(block(0), block(2), first_ss, tok_rs.at[2], low)
     to_low.start()
 
-    def to_z(d):
-        return remote(block(0), block(near[d]), first_ss.at[d], tok_rs.at[near[d]], along_z(4 - d))
-
-    to_z(1).start()
-
-    def relay(d):
-        return remote(block(2), block(2 + d), relay_ss.at[d - 1], tok_rs.at[2 + d], along_z(4 - d))
+    def along(side, d, u=None):
+        src = 2 * side
+        if d == 2:
+            r = 6 - 2 * side
+            return remote(block(src), block(r), z_ss.at[side, 4], tok_rs.at[r], along_z(2))
+        r, i = ((1, 7), (3, 5))[side][u], d // 2
+        return remote(tok.at[src, u, own_rows], tok.at[r, i, own_rows], z_ss.at[side, 2 * i + u], tok_rs.at[r], along_z(4 - d))
+
+    along(0, 1, 0).start()
+    along(0, 3, 0).start()
 
     def take(r):
         remote(block(r), block(r), fwd_ss.at[r], tok_rs.at[r], low).wait_recv()
@@ -128,14 +129,24 @@
         def _():
             take(1)
             take(2)
-            for d in (1, 3, 2):
-                relay(d).start()
-            for d in (3, 2):
-                to_z(d).start()
+            along(1, 1, 0).start()
+            along(1, 3, 0).start()
+            along(1, 2).start()
 
         @pl.when((p > 1) & (p < GROUPS - 1))
         def _():
             take(p + 1)
+
+        @pl.when(p == 2)
+        def _():
+            along(1, 1, 1).start()
+            along(1, 3, 1).start()
+            along(0, 2).start()
+
+        @pl.when(p == 3)
+        def _():
+            along(0, 1, 1).start()
+            along(0, 3, 1).start()
 
     def x1_copy(k, h):
         return remote(x1s.at[k, h], x1r.at[k, h], x1_ss.at[k, h], x1_rs.at[k, h], dest1[h])
@@ -253,53 +264,64 @@
                 gx_copy(2 * r + u, h).wait_send()
                 gy_copy(2 * r + u, h).wait_send()
 
-    def o_copy(m, i):
-        r, c = (m + 1) % GROUPS, pl.ds(i * PAIR, PAIR)
-        far = (r + 2) // 4 % 2
-        return remote(osend.at[m % 2, :, :, c], orecv.at[r, :, :, c], o_ss.at[m % 2, i], o_rs.at[r, i], along_z((r + 2 * far) % 4))
+    def o_copy(m, u):
+        r = (m + 1) % GROUPS
+        d = 2 + r % 2 * (2 * u - 1)
+        return remote(osend.at[m % 2, u], orecv.at[r, u], o_ss.at[m % 2, u], o_rs.at[r, u], along_z(d))
 
     def send_out(m):
         r = (m + 1) % GROUPS
         for i in (0, 1):
-            c = pl.ds(i * PAIR, PAIR)
             c_copy(m, i).wait_recv()
 
-            @pl.when((m == 1) | (m == 7))
-            def _():
-                acc[m // 4, :, :, c] = po[m % 2, :, own_rows, c] + cr[r, :, :, c]
-
-            @pl.when((m != 1) & (m != 7))
-            def _():
+        @pl.when((m == 1) | (m == 7))
+        def _():
+            acc[m // 4] = po[m % 2, :, own_rows] + cr[r]
+
+        @pl.when((m != 1) & (m != 7))
+        def _():
+            for u in (0, 1):
                 @pl.when(m == 2)
                 def _():
-                    o_copy(0, i).wait_send()
+                    o_copy(0, u).wait_send()
 
                 @pl.when(m >= 4)
                 def _():
-                    o_copy(m - 2, i).wait_send()
-
-                osend[m % 2, :, :, c] = code(po[m % 2, :, own_rows, c] + cr[r, :, :, c], OUT_SCALE)
-                o_copy(m, i).start()
+                    o_copy(m - 2, u).wait_send()
+
+                osend[m % 2, u] = code(po[m % 2, u, own_rows] + cr[r, u], OUT_SCALE)
+                o_copy(m, u).start()
 
         to_sibling(r).wait_send()
         for u in (0, 1):
             for h in (0, 1):
                 gxx_copy(2 * r + u, h).wait_send()
 
-    y2_copy = remote(y2s, y2r, y2_ss, y2_rs, low)
+    def y2_copy(u):
+        return remote(y2s.at[u], y2r.at[u], y2_ss.at[u], y2_rs.at[u], low)
+
+    def others(u, a, b, c):
+        r = c if u else a
+        for i in (0, 1):
+            o_copy(r - 1, i).wait_recv()
+        o_copy(b - 1, u).wait_recv()
+        return decode(orecv[r, 0], OUT_SCALE) + decode(orecv[r, 1], OUT_SCALE) + decode(orecv[b, u], OUT_SCALE)
 
     def cross(m):
+        for u in (0, 1):
+            @pl.when(m == 3 + u)
+            def _():
+                y2s[u] = code(acc[0, u] + others(u, 3, 4, 5), OUT_SCALE)
+                y2_copy(u).start()
+
         @pl.when(m == 4)
         def _():
-            for r in (3, 4, 5):
-                for i in (0, 1):
-                    o_copy(r - 1, i).wait_recv()
-            y2s[...] = code(acc[0] + sum(decode(orecv[r], OUT_SCALE) for r in (3, 4, 5)), OUT_SCALE)
-            y2_copy.start()
             to_low.wait_send()
-            for d in (1, 2, 3):
-                to_z(d).wait_send()
-                relay(d).wait_send()
+            for side in (0, 1):
+                for d in (1, 3):
+                    for u in (0, 1):
+                        along(side, d, u).wait_send()
+                along(side, 2).wait_send()
 
     tasks = dict(first=first, pass_on=pass_on, sum_x=sum_x, sum_y=sum_y, activate=activate, gather_y=gather_y,
                  gather_x=gather_x, second=second, send_out=send_out, cross=cross)
@@ -320,19 +342,18 @@
 
     lax.fori_loop(0, STEPS, step, 0)
 
-    for r in (1, 6, 7):
-        for i in (0, 1):
-            o_copy(r - 1, i).wait_recv()
-    y2_copy.wait_recv()
-    far = sum(decode(orecv[r], OUT_SCALE) for r in (1, 6, 7))
-    out_ref[...] = acc[1] + far + decode(y2r[...], OUT_SCALE) + bias_out[...]
+    for u in (0, 1):
+        y2_copy(u).wait_recv()
+        rest = acc[1, u] + decode(y2r[u], OUT_SCALE) + bias_out[...]
+        out_ref[u] = rest + others(u, 1, 6, 7)
 
     for i in (0, 1):
         for m in (GROUPS - 2, GROUPS - 1):
             c_copy(m, i).wait_send()
         for m in (5, 6):
             o_copy(m, i).wait_send()
-    y2_copy.wait_send()
+    for u in (0, 1):
+        y2_copy(u).wait_send()
 
 
 def per_device(tokens, w_in, b_in, w_out, b_out):
@@ -347,10 +368,10 @@
         pltpu.VMEM((n, SLOT, FF), BF16), pltpu.VMEM((2, 2, SLOT, D), F32), pltpu.VMEM((g, 2, HALF, D), F32),
         pltpu.VMEM((2, 2, HALF, D), BF16), pltpu.VMEM((g, 2, HALF, D), BF16), pltpu.VMEM((2, 2, HALF, D), F32),
         pltpu.VMEM((2, HALF, D), BF16), pltpu.VMEM((2, HALF, D), BF16),
-        dma((4,)), dma, dma((2,)), dma, dma((4,)), dma((g,)), dma((3,)), dma((g,)), dma((g,)),
+        dma((4,)), dma, dma((2,)), dma, dma, dma((g,)), dma((2, 5)), dma((g,)), dma((g,)),
         dma((n, 2)), dma((n, 2)), dma((n, 2)), dma((n, 2)), dma((n, 2)), dma((n, 2)),
         dma((n, 2)), dma((n, 2)), dma((n, 2)), dma((n, 2)), dma((n, 2)), dma((n, 2)),
-        dma((2, 2)), dma((g, 2)), dma((2, 2)), dma((g, 2)), dma, dma,
+        dma((2, 2)), dma((g, 2)), dma((2, 2)), dma((g, 2)), dma((2,)), dma((2,)),
     ]
     out = pl.pallas_call(
         kernel,

time: 113 us -> 110 us (0.973)
  Pallas kernels: 111 us -> 109 us
    pallas_call x1, Pallas kernels: 111 us -> 109 us  [per_device(): pl.pallas_call(kernel, out_shape=pltpu.VMEM((2, HALF, D), F32), in_specs=...]
where the time goes in v6:
time: 110 us; the launch traced here: 109 us
  Pallas kernels  109 us (99%)
    pallas_call x1, Pallas kernels, per_device(): pl.pallas_call(kernel, out_shape=pltpu.VMEM((2, HALF, D), F32), in_specs=...  109 us

profile of v6, /device:TPU:1, one launch (start us, length us, event | category | flops | bytes accessed | tf_op | source)
XLA Modules:
  0.0 109.3 jit_solution(4503382520193162732)
XLA Ops:
  0.0 108.5 %shard_map.55 = f32[2,32,1536]{2,1,0:T(8,128)S(1)} custom-call(bf16[2,32,1536]{2,1,0:T(8,128)(2,1)} %bitcast.3, bf16[1536,3072]{1,0:T(8,128)(2,1)} %w1_hbm.1, bf16[3072]{0:T(1024)(128)(2,1)} %bin_hbm.1, bf16[3072,1536]{1,0:T(8,128)(2,1)} %w2_hbm.1, bf16[1536]{0:T(1024)(128)(2,1)} %bout_hbm.1), custom_call_target="tpu_custom_call" | custom-call | flops 19327352832 | bytes 18874368 | tf_op jit(solution)/shard_map/pallas_call | solution.py:376
  108.5 0.7 copy.7

commit v7 on v6

--- a/solution.py
+++ b/solution.py
@@ -15,11 +15,11 @@
 HIDDEN_SCALE, OUT_SCALE = 2.0**20, 2.0**9
 
 ORDER = (
-    ("send_out", 12), ("pass_on", 0), ("first", 0), ("second", 11), ("activate0", 4), ("sum_x0", 1), ("activate1", 4),
-    ("gather_x0", 9), ("sum_y0", 2), ("sum_x1", 1), ("cross", 13), ("gather_x1", 8), ("gather_y0", 7), ("sum_y1", 2),
-    ("gather_y1", 6),
+    ("gather_y0", 6), ("first", 0), ("gather_x1", 8), ("sum_x0", 1), ("sum_y0", 2), ("cross", 12), ("sum_x1", 1),
+    ("send_out", 10), ("pass_on", -1), ("activate0", 3), ("gather_y1", 6), ("gather_x0", 7), ("second", 9),
+    ("sum_y1", 2), ("activate1", 3),
 )
-STEPS = 20
+STEPS = 18
 
 
 def code(v, scale):
@@ -35,7 +35,7 @@
 
 def kernel(tok_hbm, w1_hbm, bin_hbm, w2_hbm, bout_hbm, out_ref,
            w1, w2, bin_raw, bout_raw, bias_in, bias_out, tok, x1s, x1r, keep, ys, yr, x2s, x2r, hid, po, cr, osend, orecv, acc, y2s, y2r,
-           w1_sem, w2_sem, bias_sem, own_sem, first_ss, tok_rs, z_ss, fwd_ss, fwd_rs,
+           w1_sem, w2_sem, bias_sem, own_sem, low_ss, low_rs, tok_rs, z_ss, fwd_ss, fwd_rs,
            x1_ss, x1_rs, y_ss, y_rs, x2_ss, x2_rs, gx_ss, gx_rs, gy_ss, gy_rs, gxx_ss, gxx_rs,
            c_ss, c_rs, o_ss, o_rs, y2_ss, y2_rs):
     row, col = lax.axis_index("row"), lax.axis_index("col")
@@ -106,8 +106,12 @@
 
     own.wait()
     to_sibling(0).start()
-    to_low = remote(block(0), block(2), first_ss, tok_rs.at[2], low)
-    to_low.start()
+
+    def to_low(u):
+        return remote(tok.at[0, u, own_rows], tok.at[2, u, own_rows], low_ss.at[u], low_rs.at[u], low)
+
+    for u in (0, 1):
+        to_low(u).start()
 
     def along(side, d, u=None):
         src = 2 * side
@@ -128,10 +132,9 @@
         @pl.when(p == 1)
         def _():
             take(1)
-            take(2)
+            to_low(0).wait_recv()
             along(1, 1, 0).start()
             along(1, 3, 0).start()
-            along(1, 2).start()
 
         @pl.when((p > 1) & (p < GROUPS - 1))
         def _():
@@ -177,6 +180,12 @@
                     x1_copy(2 * r + u, h).start()
                 else:
                     keep[2 * r + u, h] = part[u * SLOT : (u + 1) * SLOT]
+
+        @pl.when(r == 1)
+        def _():
+            to_low(1).wait_recv()
+            to_sibling(2).start()
+            along(1, 2).start()
 
     def y_copy(k, h):
         return remote(ys.at[k, h], yr.at[k, h], y_ss.at[k, h], y_rs.at[k, h], across)
@@ -316,7 +325,8 @@
 
         @pl.when(m == 4)
         def _():
-            to_low.wait_send()
+            for u in (0, 1):
+                to_low(u).wait_send()
             for side in (0, 1):
                 for d in (1, 3):
                     for u in (0, 1):
@@ -368,7 +378,7 @@
         pltpu.VMEM((n, SLOT, FF), BF16), pltpu.VMEM((2, 2, SLOT, D), F32), pltpu.VMEM((g, 2, HALF, D), F32),
         pltpu.VMEM((2, 2, HALF, D), BF16), pltpu.VMEM((g, 2, HALF, D), BF16), pltpu.VMEM((2, 2, HALF, D), F32),
         pltpu.VMEM((2, HALF, D), BF16), pltpu.VMEM((2, HALF, D), BF16),
-        dma((4,)), dma, dma((2,)), dma, dma, dma((g,)), dma((2, 5)), dma((g,)), dma((g,)),
+        dma((4,)), dma, dma((2,)), dma, dma((2,)), dma((2,)), dma((g,)), dma((2, 5)), dma((g,)), dma((g,)),
         dma((n, 2)), dma((n, 2)), dma((n, 2)), dma((n, 2)), dma((n, 2)), dma((n, 2)),
         dma((n, 2)), dma((n, 2)), dma((n, 2)), dma((n, 2)), dma((n, 2)), dma((n, 2)),
         dma((2, 2)), dma((g, 2)), dma((2, 2)), dma((g, 2)), dma((2,)), dma((2,)),

time: 110 us -> 108 us (0.982)
  Pallas kernels: 109 us -> 107 us
    pallas_call x1, Pallas kernels: 109 us -> 107 us  [per_device(): pl.pallas_call(kernel, out_shape=pltpu.VMEM((2, HALF, D), F32), in_specs=...]
where the time goes in v7:
time: 108 us
  Pallas kernels  107 us (99%)
    pallas_call x1, Pallas kernels, per_device(): pl.pallas_call(kernel, out_shape=pltpu.VMEM((2, HALF, D), F32), in_specs=...  107 us

profile of v7, /device:TPU:1, one launch (start us, length us, event | category | flops | bytes accessed | tf_op | source)
XLA Modules:
  0.0 107.9 jit_solution(16220266478063519566)
XLA Ops:
  0.0 107.2 %shard_map.55 = f32[2,32,1536]{2,1,0:T(8,128)S(1)} custom-call(bf16[2,32,1536]{2,1,0:T(8,128)(2,1)} %bitcast.3, bf16[1536,3072]{1,0:T(8,128)(2,1)} %w1_hbm.1, bf16[3072]{0:T(1024)(128)(2,1)} %bin_hbm.1, bf16[3072,1536]{1,0:T(8,128)(2,1)} %w2_hbm.1, bf16[1536]{0:T(1024)(128)(2,1)} %bout_hbm.1), custom_call_target="tpu_custom_call" | custom-call | flops 19327352832 | bytes 18874368 | tf_op jit(solution)/shard_map/pallas_call | solution.py:386
  107.2 0.7 copy.7

commit v8 on v7

--- a/solution.py
+++ b/solution.py
@@ -15,9 +15,9 @@
 HIDDEN_SCALE, OUT_SCALE = 2.0**20, 2.0**9
 
 ORDER = (
-    ("gather_y0", 6), ("first", 0), ("gather_x1", 8), ("sum_x0", 1), ("sum_y0", 2), ("cross", 12), ("sum_x1", 1),
-    ("send_out", 10), ("pass_on", -1), ("activate0", 3), ("gather_y1", 6), ("gather_x0", 7), ("second", 9),
-    ("sum_y1", 2), ("activate1", 3),
+    ("gather_y0", 6), ("first", 0), ("gather_x0", 8), ("sum_x0", 1), ("second", 10), ("sum_y1", 3), ("activate1", 4),
+    ("gather_x1", 8), ("cross", 12), ("sum_x1", 1), ("sum_y0", 2), ("send_out", 10), ("pass_on", -1),
+    ("activate0", 3), ("gather_y1", 6),
 )
 STEPS = 18
 

time: 108 us -> 107 us (level)
  no operation moved by 1% of the time
where the time goes in v8:
time: 107 us
  Pallas kernels  106 us (99%)
    pallas_call x1, Pallas kernels, per_device(): pl.pallas_call(kernel, out_shape=pltpu.VMEM((2, HALF, D), F32), in_specs=...  106 us

profile of v8, /device:TPU:1, one launch (start us, length us, event | category | flops | bytes accessed | tf_op | source)
XLA Modules:
  0.0 107.1 jit_solution(2565741636261226117)
XLA Ops:
  0.0 106.3 %shard_map.55 = f32[2,32,1536]{2,1,0:T(8,128)S(1)} custom-call(bf16[2,32,1536]{2,1,0:T(8,128)(2,1)} %bitcast.3, bf16[1536,3072]{1,0:T(8,128)(2,1)} %w1_hbm.1, bf16[3072]{0:T(1024)(128)(2,1)} %bin_hbm.1, bf16[3072,1536]{1,0:T(8,128)(2,1)} %w2_hbm.1, bf16[1536]{0:T(1024)(128)(2,1)} %bout_hbm.1), custom_call_target="tpu_custom_call" | custom-call | flops 19327352832 | bytes 18874368 | tf_op jit(solution)/shard_map/pallas_call | solution.py:386
  106.3 0.7 copy.7

commit v9 on v8

--- a/solution.py
+++ b/solution.py
@@ -260,13 +260,21 @@
             for i in (0, 1):
                 c_copy(m - 2, i).wait_send()
 
+        def product(pairs, c):
+            return sum(
+                jnp.dot(hid[pl.ds(2 * r, 2), :, cols(p, PAIR)].reshape(ROWS, PAIR), w2[cols(p, PAIR), c], preferred_element_type=F32)
+                for p in pairs
+            ).reshape(2, SLOT, PAIR)
+
+        for i in (0, 1):
+            c = pl.ds(i * PAIR, PAIR)
+            po[m % 2, :, :, c] = product(pair_of, c)
         for u in (0, 1):
             for h in (0, 1):
                 gxx_copy(2 * r + u, h).wait_recv()
-        hidden = hid[pl.ds(2 * r, 2)].reshape(ROWS, FF)
         for i in (0, 1):
             c = pl.ds(i * PAIR, PAIR)
-            po[m % 2, :, :, c] = jnp.dot(hidden, w2[:, c], preferred_element_type=F32).reshape(2, SLOT, PAIR)
+            po[m % 2, :, :, c] += product(other_pair, c)
             c_copy(m, i).start()
         for u in (0, 1):
             for h in (0, 1):

time: 107 us -> 107 us (level)
  no operation moved by 1% of the time
where the time goes in v9:
time: 107 us; the launch traced here: 106 us
  Pallas kernels  106 us (99%)
    pallas_call x1, Pallas kernels, per_device(): pl.pallas_call(kernel, out_shape=pltpu.VMEM((2, HALF, D), F32), in_specs=...  106 us

profile of v9, /device:TPU:1, one launch (start us, length us, event | category | flops | bytes accessed | tf_op | source)
XLA Modules:
  0.0 106.5 jit_solution(6043433848470575945)
XLA Ops:
  0.0 105.7 %shard_map.55 = f32[2,32,1536]{2,1,0:T(8,128)S(1)} custom-call(bf16[2,32,1536]{2,1,0:T(8,128)(2,1)} %bitcast.3, bf16[1536,3072]{1,0:T(8,128)(2,1)} %w1_hbm.1, bf16[3072]{0:T(1024)(128)(2,1)} %bin_hbm.1, bf16[3072,1536]{1,0:T(8,128)(2,1)} %w2_hbm.1, bf16[1536]{0:T(1024)(128)(2,1)} %bout_hbm.1), custom_call_target="tpu_custom_call" | custom-call | flops 19327352832 | bytes 18874368 | tf_op jit(solution)/shard_map/pallas_call | solution.py:394
  105.7 0.7 copy.7
